TPU v7x, 512 devices: a whole 4x8x8 slice. The times are simulated.
512 devices in a mesh: dap: 64 (over y, x, z_hi), dp: 8 (over z_lo, core).
Axes of the slice: x: 4, y: 8, z: 8 (z_hi: 2, z_lo: 4; z = z_hi * 4 + z_lo), core: 2. Of those that a mesh axis runs over, the one named last changes fastest.
Arguments:
- homolog_tensor: bfloat16 [2048, 512, 256], P(('dp', 'dap')), parts along dimension 0, may hold values from -6 to 6
- couple_tensor: bfloat16 [4096, 512, 128], P(('dp', 'dap')), parts along dimension 0, may hold values from -6 to 6
- homolog_presence: int32 [2048, 512], P(('dp', 'dap')), parts along dimension 0, may hold values 0 or 1
- asking_matrix: bfloat16 [256, 256], replicated, may hold values from -0.71875 to 0.71875
- lookup_matrix: bfloat16 [256, 256], replicated, may hold values from -0.71875 to 0.71875
- content_matrix: bfloat16 [256, 256], replicated, may hold values from -0.375 to 0.375
- sigmoid_matrix: bfloat16 [256, 256], replicated, may hold values from -0.375 to 0.375
- sigmoid_offset: bfloat16 [256], replicated, may hold values from -4 to 4
- attention_final_matrix: bfloat16 [256, 256], replicated, may hold values from -0.75 to 0.75
- first_factor_matrix: bfloat16 [256, 32], replicated, may hold values from -0.375 to 0.375
- second_factor_matrix: bfloat16 [256, 32], replicated, may hold values from -0.375 to 0.375
- tensor_product_matrix: bfloat16 [1024, 128], replicated, may hold values from -3 to 3
- couple_offset_matrix: bfloat16 [128, 8], replicated, may hold values from -40 to 40
Outputs:
- homolog_revised: bfloat16 [2048, 512, 256], P(('dp', 'dap')), parts along dimension 0
- pair_updated: bfloat16 [4096, 512, 128], P(('dp', 'dap')), parts along dimension 0
There are 8 independent parts, one for each index of `dp`. A program takes and returns all parts, laid end to end along the dimension named above; an argument that names none is the same for every part. Nothing has to cross between parts.
All inputs are finite; a program needn't handle non-finite values. No bound on the sum of `homolog_presence` on one device may be relied on, other than what follows from the above.
Results may differ from a plain program's by a relative error of at most 0.012.
The roundings to bfloat16 on the way count: a program that leaves them out, or rounds other values in their place, can miss the bound.
Values may be sent and summed in bfloat16 or wider, within the bound.
A program may use at most 128 MiB of HBM per device.

v0:
```python
import jax
import jax.numpy as jnp
from jax import lax
from jax.sharding import PartitionSpec as P

CZ = 128
ATTENTION_HEADS = 8
PER_HEAD_WIDTH = 32
PROJECTED_WIDTH = 32


def standardize_features(values):
    mean = jnp.mean(values, axis=-1, keepdims=True)
    centered = values - mean
    variance = jnp.mean(centered * centered, axis=-1, keepdims=True)
    return centered * lax.rsqrt(variance + 1e-05)


def outer_block(left_rows, mask_rows, right_piece, mask_piece, tensor_product_matrix):
    res_dev = left_rows.shape[1]
    count = right_piece.shape[1]
    outer = jnp.einsum(
        "sic,sjd->ijcd", left_rows, right_piece, preferred_element_type=jnp.float32
    ).astype(jnp.bfloat16)
    projected = jnp.dot(
        outer.reshape(res_dev * count, PROJECTED_WIDTH * PROJECTED_WIDTH),
        tensor_product_matrix,
        preferred_element_type=jnp.float32,
    )
    projected = projected.reshape(res_dev, count, CZ)
    counts = lax.dot_general(
        mask_rows, mask_piece, (((0,), (0,)), ((), ())), preferred_element_type=jnp.float32
    )
    return projected / (counts + 0.001)[..., None]


def on_device(
    homolog_tensor,
    couple_tensor,
    homolog_presence,
    asking_matrix,
    lookup_matrix,
    content_matrix,
    sigmoid_matrix,
    sigmoid_offset,
    attention_final_matrix,
    first_factor_matrix,
    second_factor_matrix,
    tensor_product_matrix,
    couple_offset_matrix,
):
    homolog_shard_index = homolog_tensor.shape[0]
    partial_total = homolog_tensor.shape[1]
    sequence_mask = homolog_presence.astype(jnp.bfloat16)
    mask_as_float = homolog_presence.astype(jnp.float32)
    standardized_lines = standardize_features(homolog_tensor.astype(jnp.float32)).astype(
        jnp.bfloat16
    )
    left_proj = (
        jnp.dot(standardized_lines, first_factor_matrix, preferred_element_type=jnp.float32)
        * mask_as_float[..., None]
    ).astype(jnp.bfloat16)
    right_proj = (
        jnp.dot(standardized_lines, second_factor_matrix, preferred_element_type=jnp.float32)
        * mask_as_float[..., None]
    ).astype(jnp.bfloat16)
    left_rows, right_rows, mask_rows = (
        lax.all_to_all(left_proj, "dap", split_axis=1, concat_axis=0, tiled=True),
        lax.all_to_all(right_proj, "dap", split_axis=1, concat_axis=0, tiled=True),
        lax.all_to_all(sequence_mask, "dap", split_axis=1, concat_axis=0, tiled=True),
    )
    update = outer_block(
        left_rows,
        mask_rows,
        lax.all_gather(right_rows, "dap", axis=1, tiled=True),
        lax.all_gather(mask_rows, "dap", axis=1, tiled=True),
        tensor_product_matrix,
    )
    pair_updated = (couple_tensor.astype(jnp.float32) + update).astype(jnp.bfloat16)
    pair_normed = standardize_features(pair_updated.astype(jnp.float32))
    bias = jnp.einsum(
        "ijc,ch->hij",
        pair_normed,
        couple_offset_matrix.astype(jnp.float32),
        precision=lax.Precision.HIGHEST,
    )
    query = (
        jnp.dot(standardized_lines, asking_matrix, preferred_element_type=jnp.float32)
        .astype(jnp.bfloat16)
        .reshape(homolog_shard_index, partial_total, ATTENTION_HEADS, PER_HEAD_WIDTH)
    )
    keys = (
        jnp.dot(standardized_lines, lookup_matrix, preferred_element_type=jnp.float32)
        .astype(jnp.bfloat16)
        .reshape(homolog_shard_index, partial_total, ATTENTION_HEADS, PER_HEAD_WIDTH)
    )
    values = (
        jnp.dot(standardized_lines, content_matrix, preferred_element_type=jnp.float32)
        .astype(jnp.bfloat16)
        .reshape(homolog_shard_index, partial_total, ATTENTION_HEADS, PER_HEAD_WIDTH)
    )
    gate = jax.nn.sigmoid(
        jnp.dot(standardized_lines, sigmoid_matrix, preferred_element_type=jnp.float32)
        + sigmoid_offset.astype(jnp.float32)
    )
    key_mask = (mask_as_float - 1.0) * 10000.0
    scale = PER_HEAD_WIDTH ** (-0.5)
    piece = lax.all_gather(bias, "dap", axis=1, tiled=True)
    count = piece.shape[1]

    def one_sequence(items):
        query_seq, key_seq, value_seq, mask_seq = items
        scores = (
            jnp.einsum("ihc,jhc->hij", query_seq, key_seq, preferred_element_type=jnp.float32)
            * scale
        )
        scores = scores + piece + mask_seq[None, None, :]
        weights = jax.nn.softmax(scores, axis=-1).astype(jnp.bfloat16)
        attended = jnp.einsum(
            "hij,jhc->ihc", weights, value_seq, preferred_element_type=jnp.float32
        )
        return attended.reshape(count, ATTENTION_HEADS * PER_HEAD_WIDTH)

    attended = lax.map(one_sequence, (query, keys, values, key_mask))
    sigmoid_scaled_result = (attended * gate).astype(jnp.bfloat16)
    homolog_revised = (
        homolog_tensor.astype(jnp.float32)
        + jnp.dot(sigmoid_scaled_result, attention_final_matrix, preferred_element_type=jnp.float32)
    ).astype(jnp.bfloat16)
    return (homolog_revised, pair_updated)


def solution(mesh):
    return jax.shard_map(
        on_device,
        mesh=mesh,
        in_specs=(
            P(("dp", "dap"), None, None),
            P(("dp", "dap"), None, None),
            P(("dp", "dap"), None),
            P(),
            P(),
            P(),
            P(),
            P(),
            P(),
            P(),
            P(),
            P(),
            P(),
        ),
        out_specs=(P(("dp", "dap"), None, None), P(("dp", "dap"), None, None)),
        check_vma=False,
    )
```

profile of v0, /device:TPU:6, one launch (start us, length us, event | category | flops | bytes accessed | tf_op | source)
XLA Modules:
  0.0 618.8 jit_solution(16578156114037828434)
XLA Ops:
  7.3 1.7 convert_reduce_fusion
  8.9 1.9 fusion.19
  10.9 1.0 fusion.25
  11.8 0.3 copy.47
  12.2 0.4 reshape.67
  12.6 31.9 %all_to_all.55 = bf16[64,2,512]{2,1,0:T(2,128)(2,1)S(1)} all-to-all(bf16[64,2,512]{2,1,0:T(2,128)(2,1)S(1)} %reshape.67), channel_id=1, replica_groups=mesh['dap'=64,'dp'=8] {'dap'}, dimensions={0} | all-to-all | bytes 262144 | tf_op jit(solution)/shard_map/all_to_all | solution.py:69
  44.9 1.0 copy.50
  46.1 0.7 copy.58
  46.8 6.5 %all-to-all-start.2 = ((bf16[4,64,8]{2,0,1:T(4,128)(2,1)}), bf16[4,64,8]{2,0,1:T(4,128)(2,1)S(1)}, u32[]{:S(2)}, u32[]{:S(2)}) async-start(bf16[4,64,8]{2,0,1:T(4,128)(2,1)} %copy.58), calls=%async_computation.2 | async-start | bytes 131072 | tf_op jit(solution)/shard_map/all_to_all | solution.py:70
  53.3 1.0 fusion.26
  54.2 0.3 copy.51
  54.6 1.1 reshape.69
  55.6 1.3 copy.46
  56.9 9.1 %all-to-all-done.2 = bf16[4,64,8]{2,0,1:T(4,128)(2,1)S(1)} async-done(((bf16[4,64,8]{2,0,1:T(4,128)(2,1)}), bf16[4,64,8]{2,0,1:T(4,128)(2,1)S(1)}, u32[]{:S(2)}, u32[]{:S(2)}) %all-to-all-start.2) | async-done | bytes 4128 | tf_op jit(solution)/shard_map/all_to_all | solution.py:70
  66.1 6.4 %all-to-all-start.1 = ((bf16[64,2,512]{2,1,0:T(2,128)(2,1)}), bf16[64,2,512]{2,1,0:T(2,128)(2,1)S(1)}, u32[]{:S(2)}, u32[]{:S(2)}) async-start(bf16[64,2,512]{2,1,0:T(2,128)(2,1)} %reshape.69), calls=%async_computation.1 | async-start | bytes 262144 | tf_op jit(solution)/shard_map/all_to_all | solution.py:68
  72.5 233.5 %all_gather.10 = bf16[256,512]{0,1:T(8,128)(2,1)S(1)} all-gather(bf16[256,8]{0,1:T(8,128)(2,1)S(1)} %copy.59), channel_id=1, replica_groups=mesh['dap'=64,'dp'=8] {'dap'}, dimensions={1}, use_global_device_ids=true | all-gather | bytes 266240 | tf_op jit(solution)/shard_map/all_gather | solution.py:76
  307.1 9.0 %convert_bitcast_fusion = bf16[8,512,32,32]{1,2,0,3:T(8,128)(2,1)} fusion(bf16[256,512,32]{0,1,2:T(8,128)(2,1)} %all-gather.3.cloned.1.call-done, bf16[256,8,32]{0,2,1:T(8,128)(2,1)S(1)} %copy.54), kind=kOutput, calls=%fused_computation.18 | convolution fusion | flops 2151677952 | bytes 16908288 | tf_op jit(solution)/shard_map/sic,sjd->ijcd/dot_general | solution.py:22
  316.0 12.0 %copy.55 = bf16[8,512,32,32]{1,3,2,0:T(8,128)(2,1)} copy(bf16[8,512,32,32]{1,2,0,3:T(8,128)(2,1)} %convert_bitcast_fusion) | data formatting | bytes 16777216 | tf_op jit(solution)/shard_map/convert_element_type | solution.py:24
  328.0 4.8 convert_reduce_fusion.1
  333.2 1.6 fusion.27
  334.9 1.5 convolution_convert_fusion
  336.4 3.0 convolution_convert_fusion.2
  339.4 2.1 convolution_convert_fusion.1
  341.5 1.3 copy.63
  342.8 189.2 %all-gather.5.cloned.1.call-done = f32[8,512,512]{2,0,1:T(8,128)} async-done(((f32[8,8,512]{2,0,1:T(8,128)}), f32[8,512,512]{2,0,1:T(8,128)}) %all-gather.5.cloned.1.call-update) | async-done | bytes 8388624 | tf_op jit(solution)/shard_map/all_gather | solution.py:108
  532.0 10.0 %copy.61 = f32[8,512,512]{1,2,0:T(8,128)} copy(f32[8,512,512]{2,0,1:T(8,128)} %all-gather.5.cloned.1.call-done) | data formatting | bytes 16777216 | tf_op jit(solution)/shard_map/while | solution.py:124
  542.0 66.3 %while.10 = (s32[]{:T(128)}, f32[4,512,256]{2,1,0:T(8,128)}, bf16[4,512,8,32]{1,3,2,0:T(8,128)(2,1)}, bf16[4,512,8,32]{1,3,2,0:T(8,128)(2,1)}, bf16[4,512,8,32]{...) while((s32[]{:T(128)}, f32[4,512,256]{2,1,0:T(8,128)}, ...), condition=%wide.region_7.8_spmd, body=%wide.region_4.7_spmd.sunk | while | flops 285217792 | bytes 78946424 | solution.py:124
  542.0 5.3 add_add_fusion.2
  547.2 1.5 fusion.72
  548.8 1.7 copy-done.2
  550.5 7.0 %fusion.73 = f32[8,32,512]{2,1,0:T(8,128)S(1)} fusion(f32[8,512]{1,0:T(8,128)S(1)} %fusion.72, f32[8,512,512]{1,2,0:T(8,128)} %copy-done.2, bf16[4,512,8,32]{1,3,2,0:T(8,128)(2,1)} %get-tuple-element.132, s32[]{:T(128)} %get-tuple-element.122), kind=kOutput, calls=%fused_computation.4.clone.1 | convolution fusion | flops 140513792 | bytes 17580544 | tf_op jit(solution)/shard_map/while/body/eval_jaxpr/hij,jhc->ihc/dot_general | solution.py:119
  557.7 0.8 constant_dynamic-update-slice_fusion.2
  558.5 5.3 add_add_fusion.2
  563.8 1.5 fusion.72
  565.3 1.7 copy-done.2
  567.0 7.0 %fusion.73 = f32[8,32,512]{2,1,0:T(8,128)S(1)} fusion(f32[8,512]{1,0:T(8,128)S(1)} %fusion.72, f32[8,512,512]{1,2,0:T(8,128)} %copy-done.2, bf16[4,512,8,32]{1,3,2,0:T(8,128)(2,1)} %get-tuple-element.132, s32[]{:T(128)} %get-tuple-element.122), kind=kOutput, calls=%fused_computation.4.clone.1 | convolution fusion | flops 140513792 | bytes 17580544 | tf_op jit(solution)/shard_map/while/body/eval_jaxpr/hij,jhc->ihc/dot_general | solution.py:119
  574.3 0.8 constant_dynamic-update-slice_fusion.2
  575.1 5.3 add_add_fusion.2
  580.4 1.5 fusion.72
  581.9 1.7 copy-done.2
  583.6 7.0 %fusion.73 = f32[8,32,512]{2,1,0:T(8,128)S(1)} fusion(f32[8,512]{1,0:T(8,128)S(1)} %fusion.72, f32[8,512,512]{1,2,0:T(8,128)} %copy-done.2, bf16[4,512,8,32]{1,3,2,0:T(8,128)(2,1)} %get-tuple-element.132, s32[]{:T(128)} %get-tuple-element.122), kind=kOutput, calls=%fused_computation.4.clone.1 | convolution fusion | flops 140513792 | bytes 17580544 | tf_op jit(solution)/shard_map/while/body/eval_jaxpr/hij,jhc->ihc/dot_general | solution.py:119
  590.8 0.8 constant_dynamic-update-slice_fusion.2
  591.7 5.3 add_add_fusion.2
  597.0 1.5 fusion.72
  598.5 1.7 copy-done.2
  600.2 7.0 %fusion.73 = f32[8,32,512]{2,1,0:T(8,128)S(1)} fusion(f32[8,512]{1,0:T(8,128)S(1)} %fusion.72, f32[8,512,512]{1,2,0:T(8,128)} %copy-done.2, bf16[4,512,8,32]{1,3,2,0:T(8,128)(2,1)} %get-tuple-element.132, s32[]{:T(128)} %get-tuple-element.122), kind=kOutput, calls=%fused_computation.4.clone.1 | convolution fusion | flops 140513792 | bytes 17580544 | tf_op jit(solution)/shard_map/while/body/eval_jaxpr/hij,jhc->ihc/dot_general | solution.py:119
  607.4 0.8 constant_dynamic-update-slice_fusion.2
  608.2 3.7 fusion.24
  (61 shorter events, 2.9 us)
Async XLA Ops:
  7.2 320.9 %copy-start = (bf16[1024,128]{1,0:T(8,128)(2,1)S(1)}, bf16[1024,128]{1,0:T(8,128)(2,1)}, u32[]{:S(2)}) copy-start(bf16[1024,128]{1,0:T(8,128)(2,1)} %param.26) | copy-start | bytes 786436
  7.2 3.7 copy-start.3
  7.2 3.6 copy-start.6
  7.2 3.7 copy-start.9
  7.2 299.8 %all-gather.3.cloned.1.call-start = ((), (), s32[]{:S(2)}) async-start(), calls=%async_computation.3 | async-start | bytes 8519680 | tf_op jit(solution)/shard_map/all_gather | solution.py:75
  12.6 40.7 %copy-start.10 = (bf16[256,32]{0,1:T(8,128)(2,1)S(1)}, bf16[256,32]{0,1:T(8,128)(2,1)}, u32[]{:S(2)}) copy-start(bf16[256,32]{0,1:T(8,128)(2,1)} %param.24) | copy-start | bytes 49156
  44.9 10.7 %copy-start.4 = (bf16[8,512,128]{2,1,0:T(8,128)(2,1)S(1)}, bf16[8,512,128]{2,1,0:T(8,128)(2,1)}, u32[]{:S(2)}) copy-start(bf16[8,512,128]{2,1,0:T(8,128)(2,1)} %param.16) | copy-start | bytes 3145732
  46.8 19.3 %all-to-all-start.2 = ((bf16[4,64,8]{2,0,1:T(4,128)(2,1)}), bf16[4,64,8]{2,0,1:T(4,128)(2,1)S(1)}, u32[]{:S(2)}, u32[]{:S(2)}) async-start(bf16[4,64,8]{2,0,1:T(4,128)(2,1)} %copy.58), calls=%async_computation.2 | async-start | bytes 131072 | tf_op jit(solution)/shard_map/all_to_all | solution.py:70
  66.1 240.2 %all-to-all-start.1 = ((bf16[64,2,512]{2,1,0:T(2,128)(2,1)}), bf16[64,2,512]{2,1,0:T(2,128)(2,1)S(1)}, u32[]{:S(2)}, u32[]{:S(2)}) async-start(bf16[64,2,512]{2,1,0:T(2,128)(2,1)} %reshape.69), calls=%async_computation.1 | async-start | bytes 262144 | tf_op jit(solution)/shard_map/all_to_all | solution.py:68
  72.4 459.6 %all-gather.5.cloned.1.call-start = ((), (), s32[]{:S(2)}) async-start(), calls=%async_computation.4 | async-start | bytes 8519680 | tf_op jit(solution)/shard_map/all_gather | solution.py:108
  316.0 12.0 %copy-start.5 = (bf16[8,512,128]{1,2,0:T(8,128)(2,1)S(1)}, bf16[8,512,128]{1,2,0:T(8,128)(2,1)}, u32[]{:S(2)}) copy-start(bf16[8,512,128]{1,2,0:T(8,128)(2,1)} %copy.46) | copy-start | bytes 3145732
  328.0 5.2 copy-start.11
  332.8 2.0 copy-start.12
  332.8 2.0 copy-start.7
  334.9 4.5 copy-start.8
  547.2 3.2 copy-start.2
  563.8 3.2 copy-start.2
  580.4 3.2 copy-start.2
  596.9 3.2 copy-start.2
  608.2 3.7 copy-start.1
Sparse Core Ops, SparseCore 0:
  46.1 231.4 all-gather.2
  335.0 196.9 all-gather.4
where the time goes:
time: 620 us; the launch traced here: 619 us
  blocking collectives  265 us (43%)
  waiting for transfers between devices  198 us (32%)
  matrix products  76.9 us (12%)
  local copies, waits for them, and re-layouts  40.7 us (7%)
  between operations  14.4 us (2%)
  starting transfers between devices  12.9 us (2%)
  other arithmetic  9.97 us (2%)
    all_gather x1, blocking collectives, on_device(): lax.all_gather(mask_rows, 'dap', axis=1, tiled=True)  234 us
    all_gather x1, waiting for transfers between devices, on_device(): piece = lax.all_gather(bias, 'dap', axis=1, tiled=True)  189 us
    all_to_all x1, blocking collectives, on_device(): lax.all_to_all(right_proj, 'dap', split_axis=1, concat_axis=0, tiled=True)  31.9 us
    dot_general x4, matrix products, one_sequence(): jnp.einsum('hij,jhc->ihc', weights, value_seq, preferred_element_type=jnp...  28.1 us
    dot_general x4, matrix products, one_sequence(): jnp.einsum('ihc,jhc->hij', query_seq, key_seq, preferred_element_type=jnp...  21.1 us
  transfers between devices with their start and end apart: 4, of which 2 were waited for; matrix products, arithmetic and copies ran while one was open for 2% of the time, Pallas kernels for 0%

commit v1 on v0

v1 whole, which is shorter than its diff:
```python
import functools
import math

import jax
import jax.numpy as jnp
from jax import lax
from jax.experimental import pallas as pl
from jax.experimental.pallas import tpu as pltpu
from jax.sharding import PartitionSpec as P

MESH = pl.DeviceIdType.MESH
F32 = jnp.float32
BF16 = jnp.bfloat16
LOG2E = math.log2(math.e)
SCORE_SCALE = 32.0**-0.5 * LOG2E
PENALTY = (56576.0, -7.46875, 0.01123046875)

NY, NX, NZ = 8, 4, 2
PLANES = 36
ROWS = 48
YZ_OFFSETS = [(dy, dz) for dz in range(NZ) for dy in range(NY) if (dy, dz) != (0, 0)]
X_OFFSETS = (1, 3, 2)


def wrap(value, size):
    return lax.rem(value + size, size)


def index_of(y, x, z):
    return (y * NX + x) * NZ + z


def remote(src, dst, send, recv, device):
    return pltpu.make_async_remote_copy(
        src_ref=src,
        dst_ref=dst,
        send_sem=send,
        recv_sem=recv,
        device_id={"dap": device},
        device_id_type=MESH,
    )


class Ring:
    def __init__(self, where, whole, half, send, recv, zsend, zrecv):
        self.y, self.x, self.z = where
        self.whole, self.half = whole, half
        self.send, self.recv = send, recv
        self.zsend, self.zrecv = zsend, zrecv

    def plane(self, part):
        return self.z if part == 0 else 1 - self.z

    def copy(self, part, way, step, block):
        view = self.half(block, self.plane(part), way) if step == 3 else self.whole(block, self.plane(part))
        to = wrap(self.y + (1 if way == 0 else -1), NY)
        return remote(
            view,
            view,
            self.send.at[part, way, step],
            self.recv.at[part, way, step],
            index_of(to, self.x, self.z),
        )

    def send_block(self, part, way, step, block):
        self.copy(part, way, step, block).start()

    def partner(self, plane):
        view = self.whole(self.y, plane)
        return remote(view, view, self.zsend, self.zrecv, index_of(self.y, self.x, 1 - self.z))

    def start(self, part):
        if part == 1:
            self.partner(1 - self.z).wait_recv()
        for way in (0, 1):
            self.send_block(part, way, 0, self.y)

    def start_partner(self):
        self.partner(self.z).start()

    def step(self, part, number):
        for way in (0, 1):
            block = wrap(self.y + (-number if way == 0 else number), NY)
            self.copy(part, way, number - 1, block).wait_recv()
            self.send_block(part, way, number, block)

    def finish(self, part):
        for way in (0, 1):
            self.copy(part, way, 3, wrap(self.y + 4, NY)).wait_recv()

    def drain(self):
        self.partner(self.z).wait_send()
        for part in (0, 1):
            for way in (0, 1):
                for step in range(4):
                    self.copy(part, way, step, self.y).wait_send()


def perform(actions):
    for action in actions:
        action()


def normalize_rows(values):
    mean = jnp.mean(values, axis=-1, keepdims=True)
    centered = values - mean
    variance = jnp.mean(centered * centered, axis=-1, keepdims=True)
    return centered * lax.rsqrt(variance + 1e-05)


def nt_dot(left, right):
    return lax.dot_general(left, right, (((1,), (1,)), ((), ())), preferred_element_type=F32)


def kernel(
    hom,
    cpl,
    mask_rows,
    mask,
    mask_wide,
    w_proj,
    gate_offset,
    w_final,
    w_left,
    w_right_t,
    w_outer_t,
    w_bias_t,
    out_hom,
    out_pair,
    normed,
    l_send,
    l_all,
    r_send,
    r_got,
    r_wide,
    r_all,
    l_wide,
    l_mixed,
    l_t,
    qkv_send,
    qkv,
    gate,
    couple,
    counts,
    outer,
    pair_send,
    bias_block,
    bias,
    penalty,
    partial,
    att_send,
    att,
    x_send,
    x_recv,
    yz_send,
    yz_recv,
    ring_send,
    ring_recv,
    z_send,
    z_recv,
    own,
):
    me = lax.axis_index("dap")
    y = lax.div(me, NX * NZ)
    x = lax.rem(lax.div(me, NZ), NX)
    z = lax.rem(me, NZ)
    yz = y * NZ + z
    where = (y, x, z)

    barrier = pltpu.get_barrier_semaphore()
    for dx in X_OFFSETS:
        pl.semaphore_signal(
            barrier, inc=1, device_id={"dap": index_of(y, wrap(x + dx, NX), z)}, device_id_type=MESH
        )
    for dy, dz in YZ_OFFSETS:
        pl.semaphore_signal(
            barrier,
            inc=1,
            device_id={"dap": index_of(wrap(y + dy, NY), x, wrap(z + dz, NZ))},
            device_id_type=MESH,
        )

    lanes = lax.broadcasted_iota(jnp.int32, (512, 128), 1)

    def project(s, total):
        lines = normalize_rows(hom[s].astype(F32)).astype(BF16)
        normed[s] = lines
        left = jnp.dot(lines, w_left[...], preferred_element_type=F32)
        right = nt_dot(w_right_t[...], lines) * mask[pl.ds(s, 1), :]
        right = right.astype(BF16)
        for k in range(NX):
            r_send[k, s, 0:32, :] = right[:, 128 * k : 128 * k + 128]
            r_send[k, s, 32:48, :] = mask_rows[s]
        return jnp.where(lax.div(lanes, 32) == s, left, total)

    left = lax.fori_loop(0, 4, project, jnp.zeros((512, 128), F32))
    left = left * mask_wide[...]
    left = left.reshape(NY, NX, NZ, 8, 128)
    for b in range(NY):
        for c in range(NZ):
            l_send[b * NZ + c] = left[b, :, c].reshape(32, 128).astype(BF16)

    pl.semaphore_wait(barrier, len(X_OFFSETS) + len(YZ_OFFSETS))

    def over_x(kind, n, src, dst):
        to = index_of(y, wrap(x + X_OFFSETS[n], NX), z)
        return remote(src, dst, x_send.at[kind, n], x_recv.at[kind, n], to)

    def to_x(n):
        return wrap(x + X_OFFSETS[n], NX)

    def from_x(n):
        return wrap(x - X_OFFSETS[n], NX)

    sent = []

    def go(copy):
        copy.start()
        sent.append(copy)

    for n in range(3):
        go(over_x(0, n, r_send.at[to_x(n)], r_got.at[x]))
    for n, (dy, dz) in enumerate(YZ_OFFSETS):
        to_y, to_z = wrap(y + dy, NY), wrap(z + dz, NZ)
        go(
            remote(
                l_send.at[to_y * NZ + to_z],
                l_all.at[x, yz],
                yz_send.at[n],
                yz_recv.at[n],
                index_of(to_y, x, to_z),
            )
        )
    for n in range(3):
        go(over_x(1, n, cpl.at[:, pl.ds(pl.multiple_of(128 * to_x(n), 128), 128), :], couple.at[x]))
    own_copies = [
        pltpu.make_async_copy(r_send.at[x], r_got.at[x], own.at[0]),
        pltpu.make_async_copy(l_send.at[yz], l_all.at[x, yz], own.at[1]),
        pltpu.make_async_copy(
            cpl.at[:, pl.ds(pl.multiple_of(128 * x, 128), 128), :], couple.at[x], own.at[2]
        ),
    ]
    for copy in own_copies:
        copy.start()

    def heads(p, carry):
        for kind in range(4):
            w = w_proj[:, 256 * kind : 256 * kind + 256]
            first = jnp.dot(normed[2 * p], w, preferred_element_type=F32)
            second = jnp.dot(normed[2 * p + 1], w, preferred_element_type=F32)
            if kind == 3:
                first = jax.nn.sigmoid(first + gate_offset[...])
                second = jax.nn.sigmoid(second + gate_offset[...])
            for k in range(NX):
                both = jnp.concatenate(
                    [first[:, 64 * k : 64 * k + 64], second[:, 64 * k : 64 * k + 64]], axis=1
                )
                if kind == 3:
                    gate[k, p] = both
                else:
                    qkv_send[k, kind, p] = both.astype(BF16)
        return carry

    own_copies[0].wait()
    for n in range(3):
        over_x(0, n, r_send.at[0], r_got.at[from_x(n)]).wait_recv()
    r_wide[...] = r_got[...].astype(F32).reshape(16 * ROWS, 128)
    rows = pl.ds(pl.multiple_of(16 * yz, 16), 16)
    for q in range(PLANES):
        r_all[q, rows, :] = r_wide[pl.ds(q, 16, stride=ROWS), :].astype(BF16)

    def r_whole(b, c):
        return r_all.at[:, pl.ds(pl.multiple_of(16 * (b * NZ + c), 16), 16), :]

    def r_half(b, c, way):
        return r_all.at[
            pl.ds(way * (PLANES // 2), PLANES // 2),
            pl.ds(pl.multiple_of(16 * (b * NZ + c), 16), 16),
            :,
        ]

    ring = Ring(
        where, r_whole, r_half, ring_send.at[0], ring_recv.at[0], z_send.at[0], z_recv.at[0]
    )
    ring.start_partner()
    ring.start(0)

    own_copies[1].wait()
    for n, (dy, dz) in enumerate(YZ_OFFSETS):
        from_yz = wrap(y - dy, NY) * NZ + wrap(z - dz, NZ)
        remote(l_send.at[0], l_all.at[x, from_yz], yz_send.at[n], yz_recv.at[n], me).wait_recv()
    for n in range(3):
        go(over_x(2, n, l_all.at[x], l_all.at[x]))

    lax.fori_loop(0, 2, heads, 0)
    ring.step(0, 1)
    ring.start(1)
    for n in range(3):
        go(over_x(3, n, qkv_send.at[to_x(n)], qkv.at[x]))
    own_qkv = pltpu.make_async_copy(qkv_send.at[x], qkv.at[x], own.at[3])
    own_qkv.start()
    ring.step(0, 2)

    for n in range(3):
        over_x(2, n, l_all.at[x], l_all.at[from_x(n)]).wait_recv()
    l_wide[...] = l_all[...].astype(F32).reshape(2048, 128)
    for pair in range(16):
        block = jnp.concatenate(
            [l_wide[pl.ds(2 * pair, 64, stride=32), :], l_wide[pl.ds(2 * pair + 1, 64, stride=32), :]],
            axis=0,
        ).T
        for e in range(2):
            l_mixed[pl.ds((2 * pair + e) * 32, 32), :] = jnp.concatenate(
                [block[32 * s : 32 * s + 32, 64 * e : 64 * e + 64] for s in range(4)], axis=1
            ).astype(BF16)
    source = lax.broadcasted_iota(jnp.int32, (256, 256), 0)
    target = lax.broadcasted_iota(jnp.int32, (256, 256), 1)
    place = lax.rem(source, 16) * 16 + lax.rem(lax.div(source, 16), 4) * 4 + lax.div(source, 64)
    order = jnp.where(place == target, 1.0, 0.0).astype(BF16)
    l_t[...] = jnp.dot(l_mixed[...], order, preferred_element_type=F32).astype(BF16)

    ring.step(1, 1)
    ring.step(0, 3)
    ring.step(1, 2)
    ring.step(1, 3)
    ring.finish(0)
    ring.finish(1)

    plane = r_all[32 + lax.div(y, 2)].astype(F32).T.astype(BF16)
    together = jnp.dot(plane, r_all[32 + x], preferred_element_type=F32).astype(BF16)
    row = lax.broadcasted_iota(jnp.int32, (32, 128), 0)
    column = lax.broadcasted_iota(jnp.int32, (32, 128), 1)
    chosen = 64 * lax.rem(y, 2) + 16 * lax.div(row, 8) + 8 * z + lax.rem(row, 8)
    pick = jnp.where(chosen == column, 1.0, 0.0).astype(BF16)
    counts[...] = 1.0 / (jnp.dot(pick, together, preferred_element_type=F32) + 0.001)

    present = jnp.concatenate([r_all[32 + k, rows, :] for k in range(4)], axis=1).astype(F32) - 1.0
    penalty[...] = (
        jnp.concatenate(
            [present * PENALTY[0], present * PENALTY[1], present * PENALTY[2], jnp.zeros((80, 512), F32)],
            axis=0,
        )
        .T.astype(BF16)
    )

    own_copies[2].wait()
    for n in range(3):
        over_x(1, n, cpl.at[:, pl.ds(0, 128), :], couple.at[from_x(n)]).wait_recv()

    def outer_rows(g, carry):
        l_rows = l_t[pl.ds(pl.multiple_of(g * 256, 256), 256), :]
        for d in range(16):
            right = jnp.concatenate([r_all[2 * d], r_all[2 * d + 1]], axis=1)
            product = jnp.dot(l_rows, right, preferred_element_type=F32).astype(BF16)
            for e in range(2):
                outer[:, (2 * d + e) * 32 : (2 * d + e) * 32 + 32, :] = product[
                    :, 128 * e : 128 * e + 128
                ].reshape(8, 32, 128)
        offsets = []
        for pair in range(4):
            right = jnp.concatenate([outer[2 * pair], outer[2 * pair + 1]], axis=1)
            update = jnp.dot(w_outer_t[...], right, preferred_element_type=F32)
            for e in range(2):
                i = 2 * pair + e
                scaled = update[:, 128 * e : 128 * e + 128] * counts[pl.ds(g * 8 + i, 1), :]
                updated = (couple[g, i].astype(F32).T + scaled).astype(BF16).astype(F32)
                pair_send[g, i] = updated.T.astype(BF16)
                mean = jnp.mean(updated, axis=0, keepdims=True)
                centered = updated - mean
                variance = jnp.mean(centered * centered, axis=0, keepdims=True)
                standard = centered * lax.rsqrt(variance + 1e-05)
                offsets.append(
                    jnp.dot(
                        w_bias_t[...],
                        standard,
                        preferred_element_type=F32,
                        precision=lax.Precision.HIGHEST,
                    )
                    * LOG2E
                )
        for h in range(8):
            bias_block[h, g] = jnp.concatenate([v[h : h + 1] for v in offsets], axis=0)
        return carry

    lax.fori_loop(0, 4, outer_rows, 0)

    columns = pl.ds(pl.multiple_of(128 * x, 128), 128)
    for n in range(3):
        go(
            over_x(
                4,
                n,
                bias_block.at[pl.ds(2 * to_x(n), 2)],
                bias.at[:, y, :, z, :, columns],
            )
        )
    own_bias = pltpu.make_async_copy(
        bias_block.at[pl.ds(2 * x, 2)], bias.at[:, y, :, z, :, columns], own.at[4]
    )
    own_bias.start()
    own_bias.wait()
    for n in range(3):
        from_columns = pl.ds(pl.multiple_of(128 * from_x(n), 128), 128)
        over_x(
            4, n, bias_block.at[pl.ds(0, 2)], bias.at[:, y, :, z, :, from_columns]
        ).wait_recv()

    def bias_ring(h):
        def whole(b, c):
            return bias.at[h, b, :, c]

        def half(b, c, way):
            return bias.at[h, b, pl.ds(2 * way, 2), c]

        return Ring(
            where,
            whole,
            half,
            ring_send.at[1 + h],
            ring_recv.at[1 + h],
            z_send.at[1 + h],
            z_recv.at[1 + h],
        )

    low, high = bias_ring(0), bias_ring(1)
    low.start_partner()
    low.start(0)
    for n in range(3):
        go(over_x(5, n, pair_send.at[to_x(n)], out_pair.at[:, columns, :]))
    own_pair = pltpu.make_async_copy(pair_send.at[x], out_pair.at[:, columns, :], own.at[5])
    own_pair.start()
    low.step(0, 1)
    low.start(1)
    low.step(0, 2)
    low.step(1, 1)
    low.step(0, 3)
    low.step(1, 2)
    high.start_partner()
    high.start(0)
    low.step(1, 3)
    high.step(0, 1)
    low.finish(0)
    low.finish(1)

    groups = lax.div(lanes, 32)
    short_lanes = lax.broadcasted_iota(jnp.int32, (256, 128), 1)

    def attend(h, owner, p, first_pass):
        keys, values = [], []
        for e in range(2):
            inside = groups == 2 * e + h
            keys.append(
                jnp.concatenate(
                    [jnp.where(inside, qkv[owner, 1, p], jnp.zeros((), BF16)), penalty[...]], axis=1
                )
            )
            values.append(
                jnp.concatenate(
                    [
                        jnp.where(inside, qkv[owner, 2, p], jnp.zeros((), BF16)),
                        jnp.where(inside, 1.0, 0.0).astype(BF16),
                    ],
                    axis=1,
                )
            )
        values = jnp.concatenate(values, axis=0)
        for part in range(2):
            chunk = slice(256 * part, 256 * part + 256)
            offset = bias[h, 4 * part : 4 * part + 4].reshape(256, 512)
            weights = []
            for e in range(2):
                number = owner * 4 + 2 * p + e
                marked = (lax.rem(short_lanes, 16) == number) & (short_lanes < 48)
                query = jnp.concatenate(
                    [qkv[owner, 0, p, chunk, :], jnp.where(marked, 1.0, 0.0).astype(BF16)], axis=1
                )
                scores = nt_dot(query, keys[e]) * SCORE_SCALE + offset
                top = jnp.max(scores, axis=-1, keepdims=True)
                weights.append(jnp.exp2(scores - top).astype(BF16))
            both = jnp.dot(jnp.concatenate(weights, axis=1), values, preferred_element_type=F32)
            active = lax.rem(lax.div(short_lanes, 32), 2) == h
            result = jnp.where(active, both[:, :128] / both[:, 128:], 0.0)
            if first_pass:
                partial[owner, p, chunk, :] = result
            else:
                att_send[owner, p, chunk, :] = (partial[owner, p, chunk, :] + result).astype(BF16)

    def run(order, h, first_pass, before, after):
        def body(n, carry):
            for k, actions in before.items():
                pl.when(n == k)(functools.partial(perform, actions))
            slot = lax.div(n, 2)
            shift = jnp.int32(order[0])
            for k in range(1, 4):
                shift = jnp.where(slot == k, order[k], shift)
            attend(h, wrap(x + shift, NX), lax.rem(n, 2), first_pass)
            for k, actions in after.items():
                pl.when(n == k)(functools.partial(perform, actions))
            return carry

        lax.fori_loop(0, 8, body, 0)

    own_qkv.wait()

    def arrive(n):
        return lambda: over_x(3, n, qkv_send.at[0], qkv.at[from_x(n)]).wait_recv()

    run(
        (0, 3, 1, 2),
        0,
        True,
        {
            0: [lambda: high.start(1)],
            1: [lambda: high.step(0, 2)],
            2: [arrive(0), lambda: high.step(1, 1)],
            3: [lambda: high.step(0, 3)],
            4: [arrive(1), lambda: high.step(1, 2)],
            5: [lambda: high.step(1, 3)],
            6: [arrive(2)],
            7: [lambda: high.finish(0), lambda: high.finish(1)],
        },
        {},
    )

    def back(n):
        return lambda: over_x(6, n, att_send.at[to_x(n)], att.at[x]).start()

    run((2, 1, 3, 0), 1, False, {}, {1: [back(2)], 3: [back(0)], 5: [back(1)]})
    own_att = pltpu.make_async_copy(att_send.at[x], att.at[x], own.at[6])
    own_att.start()
    own_att.wait()
    for n in (2, 0, 1):
        over_x(6, n, att_send.at[0], att.at[from_x(n)]).wait_recv()

    nothing = jnp.zeros((64, 256), BF16)
    finals = []
    for e in range(2):
        parts = []
        for k in range(NX):
            piece = w_final[64 * k : 64 * k + 64, :]
            parts += [piece, nothing] if e == 0 else [nothing, piece]
        finals.append(jnp.concatenate(parts, axis=0))
    for p in range(2):
        gated = jnp.concatenate(
            [(att[k, p].astype(F32) * gate[k, p]).astype(BF16) for k in range(NX)], axis=1
        )
        for e in range(2):
            s = 2 * p + e
            out_hom[s] = (
                hom[s].astype(F32) + jnp.dot(gated, finals[e], preferred_element_type=F32)
            ).astype(BF16)

    own_pair.wait()
    for n in range(3):
        over_x(
            5,
            n,
            pair_send.at[0],
            out_pair.at[:, pl.ds(pl.multiple_of(128 * from_x(n), 128), 128), :],
        ).wait_recv()
    for n in range(3):
        over_x(6, n, att_send.at[to_x(n)], att.at[x]).wait_send()
    for copy in sent:
        copy.wait_send()
    for one in (ring, low, high):
        one.drain()


def on_device(
    homolog_tensor,
    couple_tensor,
    homolog_presence,
    asking_matrix,
    lookup_matrix,
    content_matrix,
    sigmoid_matrix,
    sigmoid_offset,
    attention_final_matrix,
    first_factor_matrix,
    second_factor_matrix,
    tensor_product_matrix,
    couple_offset_matrix,
):
    mask = homolog_presence.astype(F32)
    mask_rows = jnp.pad(
        homolog_presence.astype(BF16).reshape(4, 4, 128), ((0, 0), (0, 12), (0, 0))
    )
    mask_wide = jnp.repeat(mask.T, 32, axis=1)
    w_proj = jnp.concatenate([asking_matrix, lookup_matrix, content_matrix, sigmoid_matrix], axis=1)
    w_left = jnp.tile(first_factor_matrix, (1, 4))
    w_outer_t = tensor_product_matrix.reshape(32, 32, 128).transpose(2, 1, 0).reshape(128, 1024)
    vmem = pl.BlockSpec(memory_space=pltpu.VMEM)
    dma = pltpu.SemaphoreType.DMA
    scratch = [
        pltpu.VMEM((4, 512, 256), BF16),
        pltpu.VMEM((16, 32, 128), BF16),
        pltpu.VMEM((4, 16, 32, 128), BF16),
        pltpu.VMEM((4, 4, ROWS, 128), BF16),
        pltpu.VMEM((4, 4, ROWS, 128), BF16),
        pltpu.VMEM((16 * ROWS, 128), F32),
        pltpu.VMEM((PLANES, 256, 128), BF16),
        pltpu.VMEM((2048, 128), F32),
        pltpu.VMEM((1024, 256), BF16),
        pltpu.VMEM((1024, 256), BF16),
        pltpu.VMEM((4, 3, 2, 512, 128), BF16),
        pltpu.VMEM((4, 3, 2, 512, 128), BF16),
        pltpu.VMEM((4, 2, 512, 128), F32),
        pltpu.VMEM((4, 8, 128, 128), BF16),
        pltpu.VMEM((32, 128), F32),
        pltpu.VMEM((8, 1024, 128), BF16),
        pltpu.VMEM((4, 8, 128, 128), BF16),
        pltpu.VMEM((8, 4, 8, 128), F32),
        pltpu.VMEM((2, 8, 4, 2, 8, 512), F32),
        pltpu.VMEM((512, 128), BF16),
        pltpu.VMEM((4, 2, 512, 128), F32),
        pltpu.VMEM((4, 2, 512, 128), BF16),
        pltpu.VMEM((4, 2, 512, 128), BF16),
        dma((7, 3)),
        dma((7, 3)),
        dma((15,)),
        dma((15,)),
        dma((3, 2, 2, 4)),
        dma((3, 2, 2, 4)),
        dma((3,)),
        dma((3,)),
        dma((7,)),
    ]
    return pl.pallas_call(
        kernel,
        name="evoformer_block",
        out_shape=(
            jax.ShapeDtypeStruct((4, 512, 256), BF16),
            jax.ShapeDtypeStruct((8, 512, 128), BF16),
        ),
        in_specs=[vmem] * 12,
        out_specs=(vmem, vmem),
        scratch_shapes=scratch,
        compiler_params=pltpu.CompilerParams(
            collective_id=1, has_side_effects=True, vmem_limit_bytes=60 << 20
        ),
    )(
        homolog_tensor,
        couple_tensor,
        mask_rows,
        mask,
        mask_wide,
        w_proj,
        sigmoid_offset.astype(F32).reshape(1, 256),
        attention_final_matrix,
        w_left,
        second_factor_matrix.T,
        w_outer_t,
        couple_offset_matrix.T.astype(F32),
    )


def solution(mesh):
    return jax.shard_map(
        on_device,
        mesh=mesh,
        in_specs=(
            P(("dp", "dap"), None, None),
            P(("dp", "dap"), None, None),
            P(("dp", "dap"), None),
            P(),
            P(),
            P(),
            P(),
            P(),
            P(),
            P(),
            P(),
            P(),
            P(),
        ),
        out_specs=(P(("dp", "dap"), None, None), P(("dp", "dap"), None, None)),
        check_vma=False,
    )
```

time: 620 us -> 137 us (0.22)
  blocking collectives: 265 us -> 0 us
  waiting for transfers between devices: 198 us -> 0 us
  Pallas kernels: 0 us -> 123 us
  matrix products: 76.9 us -> 0 us
  local copies, waits for them, and re-layouts: 40.7 us -> 7.01 us
  between operations: 14.4 us -> 0.71 us
  starting transfers between devices: 12.9 us -> 0 us
    all_gather x1 -> x0, blocking collectives: 234 us -> none  [on_device(): lax.all_gather(mask_rows, 'dap', axis=1, tiled=True)]
    all_gather x2 -> x0, waiting for transfers between devices: 189 us -> none  [the longest x1 189 us: on_device(): piece = lax.all_gather(bias, 'dap', axis=1, tiled=True)]
    pallas_call x0 -> x1, Pallas kernels: none -> 123 us  [on_device(): pl.pallas_call(kernel, name='evoformer_block', out_shape=(jax.ShapeDtypeS...]
    dot_general x18 -> x0, matrix products: 76.9 us -> none  [the longest x4 28.1 us: one_sequence(): jnp.einsum('hij,jhc->ihc', weights, value_seq, preferred_element_type=jnp...]
    all_to_all x1 -> x0, blocking collectives: 31.9 us -> none  [on_device(): lax.all_to_all(right_proj, 'dap', split_axis=1, concat_axis=0, tiled=True)]
    while x9 -> x0, local copies, waits for them, and re-layouts: 16.7 us -> none  [the longest x1 9.96 us: on_device(): attended = lax.map(one_sequence, (query, keys, values, key_mask))]
    all_to_all x2 -> x0, starting transfers between devices: 12.8 us -> none  [the longest x1 6.47 us: on_device(): lax.all_to_all(sequence_mask, 'dap', split_axis=1, concat_axis=0, tiled=T...]
    convert_element_type x3 -> x0, local copies, waits for them, and re-layouts: 12.6 us -> none  [the longest x1 12 us: outer_block(): outer = jnp.einsum('sic,sjd->ijcd', left_rows, right_piece, preferred_ele...]
  transfers between devices with their start and end apart: 4 -> 0, of which waited for: 2 -> 0; matrix products, arithmetic and copies ran while one was open for 2% -> 0% of each run, Pallas kernels for 0% -> 0%
where the time goes in v1:
time: 137 us; the launch traced here: 135 us
  Pallas kernels  123 us (90%)
  local copies, waits for them, and re-layouts  7.01 us (5%)
  other arithmetic  3.96 us (3%)
    pallas_call x1, Pallas kernels, on_device(): pl.pallas_call(kernel, name='evoformer_block', out_shape=(jax.ShapeDtypeS...  123 us
    unnamed x18, local copies, waits for them, and re-layouts  3.85 us

profile of v1, /device:TPU:6, one launch (start us, length us, event | category | flops | bytes accessed | tf_op | source)
XLA Modules:
  0.0 135.1 jit_solution(36444275042944095)
XLA Ops:
  0.6 0.0 copy-start.7
  0.6 1.2 reshape.31
  1.9 1.3 convert_bitcast_fusion.w_bias_t
  3.1 0.0 copy-done.7
  3.1 0.6 convert_bitcast_fusion.1
  3.7 0.0 copy-start.6
  3.8 0.6 pad.4.mask_rows
  4.4 0.1 copy-done.6
  4.5 0.7 copy.23.w_left
  5.2 0.0 copy-start.1
  5.2 0.8 copy.22.mask_wide
  6.1 0.1 copy-done.1
  6.2 0.1 copy.21
  6.3 0.0 copy-start.2
  6.3 0.0 copy-start.3
  6.3 0.0 copy-start.4
  6.3 0.0 copy-start.5
  6.3 0.8 copy.24.w_outer_t
  7.2 0.0 copy-done.2
  7.2 0.1 copy-done.3
  7.3 0.1 copy-done.4
  7.3 0.2 copy-done.5
  7.5 0.9 pad_maximum_fusion.w_proj
  8.3 123.4 %evoformer_block.1 = (bf16[4,512,256]{2,1,0:T(8,128)(2,1)}, bf16[8,512,128]{2,1,0:T(8,128)(2,1)}) custom-call(bf16[4,512,256]{2,1,0:T(8,128)(2,1)} %hom.1, bf16[8,512,128]{2,1,0:T(8,128)(2,1)} %cpl.1, bf16[4,16,128]{2,1,0:T(8,128)(2,1)} %pad.4.mask_rows, f32[4,512]{1,0:T(4,128)} %get-tuple-element.3.mask, f32[512,128]{1,0:T(8,128)} %copy.22.mask_wide, ...), custom_call_target="tpu_custom_call" | custom-call | tf_op jit(solution)/shard_map/evoformer_block/pallas_call | solution.py:628
  131.8 0.0 copy-start
  131.8 2.4 %copy.27 = bf16[4,512,256]{2,1,0:T(8,128)(2,1)} copy(bf16[4,512,256]{2,1,0:T(8,128)(2,1)} %get-tuple-element.7) | data formatting | bytes 2097152
  134.1 0.0 copy-done
  134.1 1.0 copy.28
  (3 shorter events, 0.0 us)
Async XLA Ops:
  0.6 2.5 %copy-start.7 = (s32[4,512]{1,0:T(4,128)S(1)}, s32[4,512]{1,0:T(4,128)}, u32[]{:S(2)}) copy-start(s32[4,512]{1,0:T(4,128)} %param.15) | copy-start | bytes 24580
  3.7 0.7 copy-start.6
  5.2 1.0 copy-start.1
  6.3 0.9 copy-start.2
  6.3 1.0 copy-start.3
  6.3 1.0 copy-start.4
  6.3 1.2 copy-start.5
  131.8 2.4 %copy-start = (bf16[8,512,128]{2,1,0:T(8,128)(2,1)S(1)}, bf16[8,512,128]{2,1,0:T(8,128)(2,1)}, u32[]{:S(2)}) copy-start(bf16[8,512,128]{2,1,0:T(8,128)(2,1)} %get-tuple-element.8) | copy-start | bytes 3145732

commit v2 on v0

v2 whole, which is shorter than its diff:
```python
import functools
import math

import jax
import jax.numpy as jnp
from jax import lax
from jax.experimental import pallas as pl
from jax.experimental.pallas import tpu as pltpu
from jax.sharding import PartitionSpec as P

MESH = pl.DeviceIdType.MESH
F32 = jnp.float32
BF16 = jnp.bfloat16
LOG2E = math.log2(math.e)
SCORE_SCALE = 32.0**-0.5 * LOG2E
PENALTY = (56576.0, -7.46875, 0.01123046875)

NY, NX, NZ = 8, 4, 2
PLANES = 36
ROWS = 48
YZ_OFFSETS = [(dy, dz) for dz in range(NZ) for dy in range(NY) if (dy, dz) != (0, 0)]
X_OFFSETS = (1, 3, 2)
XZ_OFFSETS = [(dx, dz) for dx in (1, 3, 2, 0) for dz in range(NZ) if (dx, dz) != (0, 0)]


def wrap(value, size):
    return lax.rem(value + size, size)


def index_of(y, x, z):
    return (y * NX + x) * NZ + z


def remote(src, dst, send, recv, device):
    return pltpu.make_async_remote_copy(
        src_ref=src,
        dst_ref=dst,
        send_sem=send,
        recv_sem=recv,
        device_id={"dap": device},
        device_id_type=MESH,
    )


class Ring:
    def __init__(self, where, whole, half, send, recv):
        self.y, self.x, self.z = where
        self.whole, self.half = whole, half
        self.send, self.recv = send, recv

    def copy(self, way, step, block):
        view = self.half(block, way) if step == 3 else self.whole(block)
        to = wrap(self.y + (1 if way == 0 else -1), NY)
        return remote(
            view, view, self.send.at[way, step], self.recv.at[way, step], index_of(to, self.x, self.z)
        )

    def start(self):
        for way in (0, 1):
            self.copy(way, 0, self.y).start()

    def step(self, number):
        for way in (0, 1):
            block = wrap(self.y + (-number if way == 0 else number), NY)
            self.copy(way, number - 1, block).wait_recv()
            self.copy(way, number, block).start()

    def finish(self):
        for way in (0, 1):
            self.copy(way, 3, wrap(self.y + 4, NY)).wait_recv()

    def drain(self):
        for way in (0, 1):
            for step in range(4):
                self.copy(way, step, self.y).wait_send()


def regroup(v0, v1, v2, v3):
    lane = lax.broadcasted_iota(jnp.int32, v0.shape, 1)
    low = lane < 64
    even = lax.rem(lax.div(lane, 32), 2) == 0
    u0 = jnp.where(low, v0, pltpu.roll(v2, 64, 1))
    u2 = jnp.where(low, pltpu.roll(v0, 64, 1), v2)
    u1 = jnp.where(low, v1, pltpu.roll(v3, 64, 1))
    u3 = jnp.where(low, pltpu.roll(v1, 64, 1), v3)
    return (
        jnp.where(even, u0, pltpu.roll(u1, 32, 1)),
        jnp.where(even, pltpu.roll(u0, 96, 1), u1),
        jnp.where(even, u2, pltpu.roll(u3, 32, 1)),
        jnp.where(even, pltpu.roll(u2, 96, 1), u3),
    )


def perform(actions):
    for action in actions:
        action()


def normalize_rows(values):
    mean = jnp.mean(values, axis=-1, keepdims=True)
    centered = values - mean
    variance = jnp.mean(centered * centered, axis=-1, keepdims=True)
    return centered * lax.rsqrt(variance + 1e-05)


def nt_dot(left, right):
    return lax.dot_general(left, right, (((1,), (1,)), ((), ())), preferred_element_type=F32)


def kernel(
    hom,
    cpl,
    presence,
    w_query,
    w_key,
    w_value,
    w_gate,
    gate_offset,
    w_left_t,
    w_right_t,
    w_outer,
    w_bias_t,
    out_gated,
    out_pair,
    normed,
    l_send,
    l_all,
    r_send,
    r_got,
    r_wide,
    r_all,
    l_wide,
    l_mixed,
    l_t,
    w_outer_wide,
    w_outer_t,
    qv_send,
    qv,
    k_send,
    k_got,
    gate,
    couple,
    couple_t,
    updated_t,
    counts,
    outer,
    pair_send,
    bias_block,
    bias,
    penalty,
    att_send,
    att,
    x_send,
    x_recv,
    xz_send,
    xz_recv,
    yz_send,
    yz_recv,
    ring_send,
    ring_recv,
    own,
):
    me = lax.axis_index("dap")
    y = lax.div(me, NX * NZ)
    x = lax.rem(lax.div(me, NZ), NX)
    z = lax.rem(me, NZ)
    yz = y * NZ + z
    where = (y, x, z)

    barrier = pltpu.get_barrier_semaphore()
    for dx, dz in XZ_OFFSETS:
        if dx != 0:
            pl.semaphore_signal(
                barrier,
                inc=1,
                device_id={"dap": index_of(y, wrap(x + dx, NX), wrap(z + dz, NZ))},
                device_id_type=MESH,
            )
    for dy, dz in YZ_OFFSETS:
        pl.semaphore_signal(
            barrier,
            inc=1,
            device_id={"dap": index_of(wrap(y + dy, NY), x, wrap(z + dz, NZ))},
            device_id_type=MESH,
        )

    def over_x(kind, n, src, dst):
        to = index_of(y, wrap(x + X_OFFSETS[n], NX), z)
        return remote(src, dst, x_send.at[kind, n], x_recv.at[kind, n], to)

    def over_xz(kind, n, src, dst):
        dx, dz = XZ_OFFSETS[n]
        to = index_of(y, wrap(x + dx, NX), wrap(z + dz, NZ))
        return remote(src, dst, xz_send.at[kind, n], xz_recv.at[kind, n], to)

    def to_xz(n):
        return wrap(x + XZ_OFFSETS[n][0], NX)

    def from_xz(n):
        dx, dz = XZ_OFFSETS[n]
        return wrap(x - dx, NX), wrap(z - dz, NZ)

    def to_x(n):
        return wrap(x + X_OFFSETS[n], NX)

    def from_x(n):
        return wrap(x - X_OFFSETS[n], NX)

    sent = []

    def go(copy):
        copy.start()
        sent.append(copy)

    def block_of(k):
        return pl.ds(pl.multiple_of(128 * k, 128), 128)

    lanes = lax.broadcasted_iota(jnp.int32, (512, 128), 1)
    groups = lax.div(lanes, 32)
    w_left = jnp.concatenate([w_left_t[...]] * 4, axis=0)

    def project(s, total):
        lines = normalize_rows(hom[s].astype(F32)).astype(BF16)
        normed[s] = lines
        left = nt_dot(lines, w_left)
        present = presence[pl.ds(s, 1), :].astype(F32)
        right = (nt_dot(w_right_t[...], lines) * present).astype(BF16)
        rows = jnp.concatenate(
            [present[:, 128 * k : 128 * k + 128] for k in range(4)] + [jnp.zeros((12, 128), F32)], axis=0
        ).astype(BF16)
        for k in range(NX):
            r_send[k, s, 0:32, :] = right[:, 128 * k : 128 * k + 128]
            r_send[k, s, 32:48, :] = rows
        return jnp.where(groups == s, left, total)

    left = lax.fori_loop(0, 4, project, jnp.zeros((512, 128), F32))
    spread = jnp.where(
        lax.div(lax.broadcasted_iota(jnp.int32, (128, 128), 1), 32)
        == lax.broadcasted_iota(jnp.int32, (128, 128), 0),
        1.0,
        0.0,
    ).astype(BF16)
    tall = jnp.concatenate([presence[...].astype(F32), jnp.zeros((124, 512), F32)], axis=0).T
    left = left * jnp.dot(tall.astype(BF16), spread, preferred_element_type=F32)
    left = left.reshape(NY, NX, NZ, 8, 128)
    for b in range(NY):
        for c in range(NZ):
            l_send[b * NZ + c] = left[b, :, c].reshape(32, 128).astype(BF16)

    pl.semaphore_wait(barrier, 6 + len(YZ_OFFSETS))

    for n in range(7):
        go(over_xz(0, n, r_send.at[to_xz(n)], r_got.at[z, x]))
    for n, (dy, dz) in enumerate(YZ_OFFSETS):
        to_y, to_z = wrap(y + dy, NY), wrap(z + dz, NZ)
        go(
            remote(
                l_send.at[to_y * NZ + to_z],
                l_all.at[x, yz],
                yz_send.at[n],
                yz_recv.at[n],
                index_of(to_y, x, to_z),
            )
        )
    for n in range(3):
        go(over_x(1, n, cpl.at[:, block_of(to_x(n)), :], couple.at[x]))
    own_copies = [
        pltpu.make_async_copy(r_send.at[x], r_got.at[z, x], own.at[0]),
        pltpu.make_async_copy(l_send.at[yz], l_all.at[x, yz], own.at[1]),
        pltpu.make_async_copy(cpl.at[:, block_of(x), :], couple.at[x], own.at[2]),
    ]
    for copy in own_copies:
        copy.start()

    def heads(part, carry):
        rows = pl.ds(pl.multiple_of(128 * part, 128), 128)
        for kind, w in enumerate((w_query, w_value, w_gate)):
            made = [jnp.dot(normed[s, rows, :], w[...], preferred_element_type=F32) for s in range(4)]
            if kind == 2:
                made = [jax.nn.sigmoid(m + gate_offset[...]) for m in made]
            for b in range(2):
                outs = regroup(*[m[:, 128 * b : 128 * b + 128] for m in made])
                for t in range(4):
                    h = 4 * b + t
                    if kind == 2:
                        gate[h // 2, h % 2, rows, :] = outs[t]
                    else:
                        qv_send[h // 2, h % 2, kind, pl.ds(2 * part, 2)] = (
                            outs[t].astype(BF16).reshape(2, 4, 16, 128)
                        )
        return carry

    w_key_t = w_key[...].astype(F32).T.astype(BF16)

    def keys(s, carry):
        made = nt_dot(w_key_t, normed[s]).astype(BF16)
        for h in range(8):
            k_send[h // 2, h % 2, pl.ds(pl.multiple_of(32 * s, 32), 32), :] = made[32 * h : 32 * h + 32]
        return carry

    lax.fori_loop(0, 4, keys, 0)
    lax.fori_loop(0, 4, heads, 0)

    def qkv_copies(h, n):
        other = from_x(n)
        return (
            (5 + 3 * h, k_send.at[to_x(n), h], k_got.at[x, h], k_got.at[other, h]),
            (6 + 3 * h, qv_send.at[to_x(n), h, 1], qv.at[x, h, 1], qv.at[other, h, 1]),
            (7 + 3 * h, qv_send.at[to_x(n), h, 0], qv.at[x, h, 0], qv.at[other, h, 0]),
        )

    def send_qkv(h, kinds=(0, 1, 2)):
        for k in kinds:
            for n in range(3):
                kind, src, dst, _ = qkv_copies(h, n)[k]
                go(over_x(kind, n, src, dst))

    def arrive_qkv(h, n):
        for kind, src, _, got in qkv_copies(h, n):
            over_x(kind, n, src, got).wait_recv()

    own_qkv = [
        pltpu.make_async_copy(k_send.at[x], k_got.at[x], own.at[3]),
        pltpu.make_async_copy(qv_send.at[x], qv.at[x], own.at[7]),
    ]
    for copy in own_qkv:
        copy.start()

    own_copies[0].wait()
    for n in range(7):
        other_x, other_z = from_xz(n)
        over_xz(0, n, r_send.at[0], r_got.at[other_z, other_x]).wait_recv()
    r_wide[...] = r_got[...].astype(F32).reshape(32 * ROWS, 128)

    def line_of(b):
        return pl.ds(pl.multiple_of(32 * b, 32), 32)

    for q in range(PLANES):
        r_all[q, line_of(y), :] = r_wide[pl.ds(q, 32, stride=ROWS), :].astype(BF16)

    def right_ring(c):
        first = (0, 18)[c]

        def whole(b):
            return r_all.at[pl.ds(first, 18), line_of(b), :]

        def half(b, way):
            return r_all.at[pl.ds(first + 9 * way, 9), line_of(b), :]

        return Ring(where, whole, half, ring_send.at[c], ring_recv.at[c])

    near, rest = right_ring(0), right_ring(1)
    near.start()
    rest.start()

    own_copies[1].wait()
    for n, (dy, dz) in enumerate(YZ_OFFSETS):
        from_yz = wrap(y - dy, NY) * NZ + wrap(z - dz, NZ)
        remote(l_send.at[0], l_all.at[x, from_yz], yz_send.at[n], yz_recv.at[n], me).wait_recv()
    for n in range(3):
        go(over_x(0, n, l_all.at[x], l_all.at[x]))
    send_qkv(0)

    w_outer_wide[...] = w_outer[...].astype(F32)
    for k in range(8):
        w_outer_t[:, 128 * k : 128 * k + 128] = (
            jnp.concatenate([w_outer_wide[pl.ds(4 * k + t, 32, stride=32), :] for t in range(4)], axis=0)
            .T.astype(BF16)
        )

    near.step(1)
    rest.step(1)

    for n in range(3):
        over_x(0, n, l_all.at[x], l_all.at[from_x(n)]).wait_recv()
    l_wide[...] = l_all[...].astype(F32).reshape(2048, 128)
    for pair in range(16):
        block = jnp.concatenate(
            [l_wide[pl.ds(2 * pair, 64, stride=32), :], l_wide[pl.ds(2 * pair + 1, 64, stride=32), :]],
            axis=0,
        ).T
        for e in range(2):
            l_mixed[pl.ds((2 * pair + e) * 32, 32), :] = jnp.concatenate(
                [block[32 * s : 32 * s + 32, 64 * e : 64 * e + 64] for s in range(4)], axis=1
            ).astype(BF16)
    source = lax.broadcasted_iota(jnp.int32, (256, 256), 0)
    target = lax.broadcasted_iota(jnp.int32, (256, 256), 1)
    place = lax.rem(source, 16) * 16 + lax.rem(lax.div(source, 16), 4) * 4 + lax.div(source, 64)
    order = jnp.where(place == target, 1.0, 0.0).astype(BF16)
    l_t[...] = jnp.dot(l_mixed[...], order, preferred_element_type=F32).astype(BF16)

    near.step(2)
    rest.step(2)

    own_copies[2].wait()
    for n in range(3):
        over_x(1, n, cpl.at[:, pl.ds(0, 128), :], couple.at[from_x(n)]).wait_recv()

    def turn_couple(g, carry):
        for i in range(8):
            couple_t[g, i] = couple[g, i].astype(F32).T
        return carry

    lax.fori_loop(0, 4, turn_couple, 0)
    near.step(3)
    send_qkv(1, (0, 1))
    rest.step(3)
    near.finish()

    def outer_rows(g, first, last):
        l_rows = l_t[pl.ds(pl.multiple_of(g * 256, 256), 256), :]
        for d in range(first, last):
            right = jnp.concatenate([r_all[2 * d], r_all[2 * d + 1]], axis=1)
            product = jnp.dot(l_rows, right, preferred_element_type=F32).astype(BF16)
            for e in range(2):
                outer[pl.ds(8 * g, 8), (2 * d + e) * 32 : (2 * d + e) * 32 + 32, :] = product[
                    :, 128 * e : 128 * e + 128
                ].reshape(8, 32, 128)

    def outer_near(g, carry):
        outer_rows(g, 0, 9)
        return carry

    lax.fori_loop(0, 4, outer_near, 0)
    rest.finish()

    plane = r_all[32 + lax.div(y, 2)].astype(F32).T.astype(BF16)
    together = jnp.dot(plane, r_all[32 + x], preferred_element_type=F32).astype(BF16)
    row = lax.broadcasted_iota(jnp.int32, (32, 128), 0)
    column = lax.broadcasted_iota(jnp.int32, (32, 128), 1)
    chosen = 64 * lax.rem(y, 2) + 16 * lax.div(row, 8) + 8 * z + lax.rem(row, 8)
    pick = jnp.where(chosen == column, 1.0, 0.0).astype(BF16)
    counts[...] = 1.0 / (jnp.dot(pick, together, preferred_element_type=F32) + 0.001)

    w_bias = jnp.concatenate([w_bias_t[...]] * 3, axis=1)

    def outer_rest(g, carry):
        outer_rows(g, 9, 16)
        offsets = []
        for pair in range(4):
            right = jnp.concatenate([outer[8 * g + 2 * pair], outer[8 * g + 2 * pair + 1]], axis=1)
            update = jnp.dot(w_outer_t[...], right, preferred_element_type=F32)
            standards = []
            for e in range(2):
                i = 2 * pair + e
                scaled = update[:, 128 * e : 128 * e + 128] * counts[pl.ds(g * 8 + i, 1), :]
                updated = (couple_t[g, i] + scaled).astype(BF16)
                updated_t[g, i] = updated
                updated = updated.astype(F32)
                mean = jnp.mean(updated, axis=0, keepdims=True)
                centered = updated - mean
                variance = jnp.mean(centered * centered, axis=0, keepdims=True)
                standards.append(centered * lax.rsqrt(variance + 1e-05))
            standard = jnp.concatenate(standards, axis=1)
            part_a = standard.astype(BF16)
            left_over = standard - part_a.astype(F32)
            part_b = left_over.astype(BF16)
            part_c = (left_over - part_b.astype(F32)).astype(BF16)
            both = (
                jnp.dot(
                    w_bias, jnp.concatenate([part_a, part_b, part_c], axis=0), preferred_element_type=F32
                )
                * LOG2E
            )
            offsets += [both[:, :128], both[:, 128:]]
        for h in range(8):
            bias_block[h, g] = jnp.concatenate([v[h : h + 1] for v in offsets], axis=0)
        return carry

    lax.fori_loop(0, 4, outer_rest, 0)

    for h in range(2):
        for n in range(7):
            go(
                over_xz(
                    1 + h, n, bias_block.at[2 * to_xz(n) + h], bias.at[h, y, :, z, :, block_of(x)]
                )
            )
    own_bias = pltpu.make_async_copy(
        bias_block.at[pl.ds(2 * x, 2)], bias.at[:, y, :, z, :, block_of(x)], own.at[4]
    )
    own_bias.start()

    present = jnp.concatenate([r_all[32 + k, pl.ds(pl.multiple_of(16 * yz, 16), 16), :] for k in range(4)], axis=1).astype(F32) - 1.0
    penalty[...] = jnp.concatenate(
        [present * PENALTY[0], present * PENALTY[1], present * PENALTY[2], jnp.zeros((80, 512), F32)],
        axis=0,
    ).astype(BF16)

    def arrive_bias(h):
        for n in range(7):
            other_x, other_z = from_xz(n)
            over_xz(
                1 + h, n, bias_block.at[0], bias.at[h, y, :, other_z, :, block_of(other_x)]
            ).wait_recv()

    def bias_ring(h, c):
        def whole(b):
            return bias.at[h, b, pl.ds(2 * c, 2)]

        def half(b, way):
            return bias.at[h, b, 2 * c + way]

        number = 2 + 2 * h + c
        return Ring(where, whole, half, ring_send.at[number], ring_recv.at[number])

    r0, r1, r2, r3 = [bias_ring(h, c) for h in range(2) for c in range(2)]
    own_bias.wait()
    arrive_bias(0)
    r0.start()
    r1.start()
    arrive_bias(1)
    r2.start()
    r3.start()
    send_qkv(1, (2,))

    def attend(h, owner, blocks):
        count = 64 * len(blocks)
        lane = lax.broadcasted_iota(jnp.int32, (count, 128), 1)
        offset = jnp.concatenate([bias[h, b].reshape(64, 512) for b in blocks], axis=0)
        query = jnp.concatenate([qv[owner, h, 0, b].reshape(64, 128) for b in blocks], axis=0)
        every = qv[owner, h, 1].reshape(512, 128)
        weights, values = [], []
        for e in range(4):
            inside = groups == e
            keys = [jnp.zeros((32, 512), BF16)] * 4
            keys[e] = k_got[owner, h, 32 * e : 32 * e + 32, :]
            key = jnp.concatenate(keys + [penalty[...]], axis=0)
            value = jnp.where(inside, every, jnp.zeros((), BF16))
            values.append(jnp.concatenate([value, jnp.where(inside, 1.0, 0.0).astype(BF16)], axis=1))
            marked = (lax.rem(lane, 16) == owner * 4 + e) & (lane < 48)
            left = jnp.concatenate([query, jnp.where(marked, 1.0, 0.0).astype(BF16)], axis=1)
            scores = jnp.dot(left, key, preferred_element_type=F32) * SCORE_SCALE + offset
            top = jnp.max(scores, axis=-1, keepdims=True)
            weights.append(jnp.exp2(scores - top).astype(BF16))
        both = jnp.dot(
            jnp.concatenate(weights, axis=1),
            jnp.concatenate(values, axis=0),
            preferred_element_type=F32,
        )
        result = (both[:, :128] / both[:, 128:]).astype(BF16).reshape(len(blocks), 4, 16, 128)
        for k, b in enumerate(blocks):
            att_send[owner, h, b] = result[k]

    def run(h, offsets, after=()):
        blocks = [wrap(y + o, NY) for o in offsets]

        def body(n, carry):
            shift = jnp.where(n == 0, 2, jnp.where(n == 1, 1, jnp.where(n == 2, 3, 0)))
            attend(h, wrap(x + shift, NX), blocks)
            for k, action in enumerate(after):
                pl.when(n == k)(action)
            return carry

        lax.fori_loop(0, 4, body, 0)

    def turn_updated(g, carry):
        for i in range(8):
            pair_send[g, i] = updated_t[g, i].astype(F32).T.astype(BF16)
        return carry

    def back(h, n):
        return lambda: over_x(3 + h, n, att_send.at[to_x(n), h], att.at[x, h]).start()

    for copy in own_qkv:
        copy.wait()
    for n in range(3):
        arrive_qkv(0, n)
    run(0, (0,))
    r0.step(1)
    r1.step(1)
    lax.fori_loop(0, 4, turn_updated, 0)
    for n in range(3):
        go(over_x(2, n, pair_send.at[to_x(n)], out_pair.at[:, block_of(x), :]))
    own_pair = pltpu.make_async_copy(pair_send.at[x], out_pair.at[:, block_of(x), :], own.at[5])
    own_pair.start()
    r2.step(1)
    r3.step(1)
    run(0, (1, -1))
    r0.step(2)
    r1.step(2)
    for n in range(3):
        arrive_qkv(1, n)
    run(1, (0, 1, -1))
    r2.step(2)
    r3.step(2)
    run(0, (2, -2))
    r0.step(3)
    r1.step(3)
    run(1, (2, -2))
    r2.step(3)
    r3.step(3)
    r0.finish()
    r1.finish()
    run(0, (3, -3, 4), (back(0, 2), back(0, 0), back(0, 1)))
    r2.finish()
    r3.finish()
    run(1, (3, -3, 4), (back(1, 2), back(1, 0), back(1, 1)))
    own_att = pltpu.make_async_copy(att_send.at[x], att.at[x], own.at[6])
    own_att.start()
    own_att.wait()
    for h in range(2):
        for n in (2, 0, 1):
            over_x(3 + h, n, att_send.at[0, h], att.at[from_x(n), h]).wait_recv()
        for k in range(NX):
            out_gated[2 * k + h] = (att[k, h].reshape(512, 128).astype(F32) * gate[k, h]).astype(BF16)

    own_pair.wait()
    for n in range(3):
        over_x(2, n, pair_send.at[0], out_pair.at[:, block_of(from_x(n)), :]).wait_recv()
    for h in range(2):
        for n in range(3):
            over_x(3 + h, n, att_send.at[to_x(n), h], att.at[x, h]).wait_send()
    for copy in sent:
        copy.wait_send()
    for one in (near, rest, r0, r1, r2, r3):
        one.drain()


def finish(gated, hom, pair, w_final, out_hom, out_pair):
    out_pair[...] = pair[...]
    quads = [regroup(*[gated[4 * b + t].astype(F32) for t in range(4)]) for b in range(2)]
    joined = jnp.concatenate(
        [jnp.concatenate([quads[0][s], quads[1][s]], axis=1).astype(BF16) for s in range(4)], axis=0
    )
    update = jnp.dot(joined, w_final[...], preferred_element_type=F32)
    out_hom[...] = (hom[...].astype(F32) + update.reshape(4, 128, 256)).astype(BF16)


def on_device(
    homolog_tensor,
    couple_tensor,
    homolog_presence,
    asking_matrix,
    lookup_matrix,
    content_matrix,
    sigmoid_matrix,
    sigmoid_offset,
    attention_final_matrix,
    first_factor_matrix,
    second_factor_matrix,
    tensor_product_matrix,
    couple_offset_matrix,
):
    vmem = pl.BlockSpec(memory_space=pltpu.VMEM)
    dma = pltpu.SemaphoreType.DMA
    scratch = [
        pltpu.VMEM((4, 512, 256), BF16),
        pltpu.VMEM((16, 32, 128), BF16),
        pltpu.VMEM((4, 16, 32, 128), BF16),
        pltpu.VMEM((4, 4, ROWS, 128), BF16),
        pltpu.VMEM((2, 4, 4, ROWS, 128), BF16),
        pltpu.VMEM((32 * ROWS, 128), F32),
        pltpu.VMEM((PLANES, 256, 128), BF16),
        pltpu.VMEM((2048, 128), F32),
        pltpu.VMEM((1024, 256), BF16),
        pltpu.VMEM((1024, 256), BF16),
        pltpu.VMEM((1024, 128), F32),
        pltpu.VMEM((128, 1024), BF16),
        pltpu.VMEM((4, 2, 2, 8, 4, 16, 128), BF16),
        pltpu.VMEM((4, 2, 2, 8, 4, 16, 128), BF16),
        pltpu.VMEM((4, 2, 128, 512), BF16),
        pltpu.VMEM((4, 2, 128, 512), BF16),
        pltpu.VMEM((4, 2, 512, 128), F32),
        pltpu.VMEM((4, 8, 128, 128), BF16),
        pltpu.VMEM((4, 8, 128, 128), F32),
        pltpu.VMEM((4, 8, 128, 128), BF16),
        pltpu.VMEM((32, 128), F32),
        pltpu.VMEM((32, 1024, 128), BF16),
        pltpu.VMEM((4, 8, 128, 128), BF16),
        pltpu.VMEM((8, 4, 8, 128), F32),
        pltpu.VMEM((2, 8, 4, 2, 8, 512), F32),
        pltpu.VMEM((128, 512), BF16),
        pltpu.VMEM((4, 2, 8, 4, 16, 128), BF16),
        pltpu.VMEM((4, 2, 8, 4, 16, 128), BF16),
        dma((11, 3)),
        dma((11, 3)),
        dma((3, 7)),
        dma((3, 7)),
        dma((15,)),
        dma((15,)),
        dma((6, 2, 4)),
        dma((6, 2, 4)),
        dma((8,)),
    ]
    gated, pair = pl.pallas_call(
        kernel,
        name="evoformer_block",
        out_shape=(
            jax.ShapeDtypeStruct((8, 512, 128), BF16),
            jax.ShapeDtypeStruct((8, 512, 128), BF16),
        ),
        in_specs=[vmem] * 12,
        out_specs=(vmem, vmem),
        scratch_shapes=scratch,
        compiler_params=pltpu.CompilerParams(
            collective_id=1, has_side_effects=True, vmem_limit_bytes=60 << 20
        ),
    )(
        homolog_tensor,
        couple_tensor,
        homolog_presence,
        asking_matrix,
        lookup_matrix,
        content_matrix,
        sigmoid_matrix,
        sigmoid_offset.astype(F32).reshape(1, 256),
        first_factor_matrix.T,
        second_factor_matrix.T,
        tensor_product_matrix,
        couple_offset_matrix.T,
    )
    rows = lambda lead, width: pl.BlockSpec((lead, 128, width), lambda i: (0, i, 0))
    return pl.pallas_call(
        finish,
        name="final_projection",
        grid=(4,),
        out_shape=(
            jax.ShapeDtypeStruct((4, 512, 256), BF16),
            jax.ShapeDtypeStruct((8, 512, 128), BF16),
        ),
        in_specs=[
            rows(8, 128),
            rows(4, 256),
            rows(8, 128),
            pl.BlockSpec((256, 256), lambda i: (0, 0)),
        ],
        out_specs=(rows(4, 256), rows(8, 128)),
    )(gated, homolog_tensor, pair, attention_final_matrix)


def solution(mesh):
    return jax.shard_map(
        on_device,
        mesh=mesh,
        in_specs=(
            P(("dp", "dap"), None, None),
            P(("dp", "dap"), None, None),
            P(("dp", "dap"), None),
            P(),
            P(),
            P(),
            P(),
            P(),
            P(),
            P(),
            P(),
            P(),
            P(),
        ),
        out_specs=(P(("dp", "dap"), None, None), P(("dp", "dap"), None, None)),
        check_vma=False,
    )
```

time: 620 us -> 115 us (0.19)
  blocking collectives: 265 us -> 0 us
  waiting for transfers between devices: 198 us -> 0 us
  Pallas kernels: 0 us -> 112 us
  matrix products: 76.9 us -> 0 us
  local copies, waits for them, and re-layouts: 40.7 us -> 0.65 us
  between operations: 14.4 us -> 0.65 us
  starting transfers between devices: 12.9 us -> 0 us
  other arithmetic: 9.97 us -> 0.56 us
    all_gather x1 -> x0, blocking collectives: 234 us -> none  [on_device(): lax.all_gather(mask_rows, 'dap', axis=1, tiled=True)]
    all_gather x2 -> x0, waiting for transfers between devices: 189 us -> none  [the longest x1 189 us: on_device(): piece = lax.all_gather(bias, 'dap', axis=1, tiled=True)]
    pallas_call x0 -> x2, Pallas kernels: none -> 112 us  [the longest x1 108 us: on_device(): pl.pallas_call(kernel, name='evoformer_block', out_shape=(jax.ShapeDtypeS...]
    dot_general x18 -> x0, matrix products: 76.9 us -> none  [the longest x4 28.1 us: one_sequence(): jnp.einsum('hij,jhc->ihc', weights, value_seq, preferred_element_type=jnp...]
    all_to_all x1 -> x0, blocking collectives: 31.9 us -> none  [on_device(): lax.all_to_all(right_proj, 'dap', split_axis=1, concat_axis=0, tiled=True)]
    while x9 -> x0, local copies, waits for them, and re-layouts: 16.7 us -> none  [the longest x1 9.96 us: on_device(): attended = lax.map(one_sequence, (query, keys, values, key_mask))]
    all_to_all x2 -> x0, starting transfers between devices: 12.8 us -> none  [the longest x1 6.47 us: on_device(): lax.all_to_all(sequence_mask, 'dap', split_axis=1, concat_axis=0, tiled=T...]
    convert_element_type x3 -> x0, local copies, waits for them, and re-layouts: 12.6 us -> none  [the longest x1 12 us: outer_block(): outer = jnp.einsum('sic,sjd->ijcd', left_rows, right_piece, preferred_ele...]
  transfers between devices with their start and end apart: 4 -> 0, of which waited for: 2 -> 0; matrix products, arithmetic and copies ran while one was open for 2% -> 0% of each run, Pallas kernels for 0% -> 0%
where the time goes in v2:
time: 115 us; the launch traced here: 114 us
  Pallas kernels  112 us (97%)
    pallas_call x1, Pallas kernels, on_device(): pl.pallas_call(kernel, name='evoformer_block', out_shape=(jax.ShapeDtypeS...  108 us
    pallas_call x1, Pallas kernels, on_device(): pl.pallas_call(finish, name='final_projection', grid=(4,), out_shape=(jax...  4.75 us

profile of v2, /device:TPU:6, one launch (start us, length us, event | category | flops | bytes accessed | tf_op | source)
XLA Modules:
  0.0 114.2 jit_solution(11935251394256806831)
XLA Ops:
  0.6 0.0 copy-start
  0.6 0.6 copy-done
  1.3 0.6 reshape.11
  1.9 107.6 %evoformer_block.1 = (bf16[8,512,128]{2,1,0:T(8,128)(2,1)}, bf16[8,512,128]{2,1,0:T(8,128)(2,1)}) custom-call(bf16[4,512,256]{2,1,0:T(8,128)(2,1)} %hom.3, bf16[8,512,128]{2,1,0:T(8,128)(2,1)} %cpl.1, s32[4,512]{1,0:T(4,128)} %presence.1, bf16[256,256]{1,0:T(8,128)(2,1)} %w_query.1, bf16[256,256]{1,0:T(8,128)(2,1)} %w_key.1, bf16[256,256]{1,0:T(8,128)(2,1)} %w_value.1, ...), custom_call_target="tpu_custom_call" | custom-call | tf_op jit(solution)/shard_map/evoformer_block/pallas_call | solution.py:686
  109.4 4.7 %final_projection.1 = (bf16[4,512,256]{2,1,0:T(8,128)(2,1)}, bf16[8,512,128]{2,1,0:T(8,128)(2,1)}) custom-call(bf16[8,512,128]{2,1,0:T(8,128)(2,1)} %get-tuple-element.4.gated, bf16[4,512,256]{2,1,0:T(8,128)(2,1)} %hom.3, bf16[8,512,128]{2,1,0:T(8,128)(2,1)} %get-tuple-element.5.pair, bf16[256,256]{1,0:T(8,128)(2,1)} %w_final.1), custom_call_target="tpu_custom_call" | custom-call | tf_op jit(solution)/shard_map/final_projection/pallas_call | solution.py:714
Async XLA Ops:
  0.6 0.7 copy-start

commit v3 on v2

--- a/solution.py
+++ b/solution.py
@@ -217,12 +217,10 @@
 
     lanes = lax.broadcasted_iota(jnp.int32, (512, 128), 1)
     groups = lax.div(lanes, 32)
-    w_left = jnp.concatenate([w_left_t[...]] * 4, axis=0)
-
-    def project(s, total):
+
+    def project_right(s, carry):
         lines = normalize_rows(hom[s].astype(F32)).astype(BF16)
         normed[s] = lines
-        left = nt_dot(lines, w_left)
         present = presence[pl.ds(s, 1), :].astype(F32)
         right = (nt_dot(w_right_t[...], lines) * present).astype(BF16)
         rows = jnp.concatenate(
@@ -231,9 +229,19 @@
         for k in range(NX):
             r_send[k, s, 0:32, :] = right[:, 128 * k : 128 * k + 128]
             r_send[k, s, 32:48, :] = rows
-        return jnp.where(groups == s, left, total)
-
-    left = lax.fori_loop(0, 4, project, jnp.zeros((512, 128), F32))
+        return carry
+
+    lax.fori_loop(0, 4, project_right, 0)
+    pl.semaphore_wait(barrier, 6 + len(YZ_OFFSETS))
+    for n in range(7):
+        go(over_xz(0, n, r_send.at[to_xz(n)], r_got.at[z, x]))
+
+    w_left = jnp.concatenate([w_left_t[...]] * 4, axis=0)
+
+    def project_left(s, total):
+        return jnp.where(groups == s, nt_dot(normed[s], w_left), total)
+
+    left = lax.fori_loop(0, 4, project_left, jnp.zeros((512, 128), F32))
     spread = jnp.where(
         lax.div(lax.broadcasted_iota(jnp.int32, (128, 128), 1), 32)
         == lax.broadcasted_iota(jnp.int32, (128, 128), 0),
@@ -247,10 +255,6 @@
         for c in range(NZ):
             l_send[b * NZ + c] = left[b, :, c].reshape(32, 128).astype(BF16)
 
-    pl.semaphore_wait(barrier, 6 + len(YZ_OFFSETS))
-
-    for n in range(7):
-        go(over_xz(0, n, r_send.at[to_xz(n)], r_got.at[z, x]))
     for n, (dy, dz) in enumerate(YZ_OFFSETS):
         to_y, to_z = wrap(y + dy, NY), wrap(z + dz, NZ)
         go(
@@ -277,7 +281,7 @@
         for kind, w in enumerate((w_query, w_value, w_gate)):
             made = [jnp.dot(normed[s, rows, :], w[...], preferred_element_type=F32) for s in range(4)]
             if kind == 2:
-                made = [jax.nn.sigmoid(m + gate_offset[...]) for m in made]
+                made = [jax.nn.sigmoid(m + offset_row) for m in made]
             for b in range(2):
                 outs = regroup(*[m[:, 128 * b : 128 * b + 128] for m in made])
                 for t in range(4):
@@ -290,6 +294,7 @@
                         )
         return carry
 
+    offset_row = gate_offset[...].astype(F32).reshape(1, 256)
     w_key_t = w_key[...].astype(F32).T.astype(BF16)
 
     def keys(s, carry):
@@ -361,6 +366,9 @@
         go(over_x(0, n, l_all.at[x], l_all.at[x]))
     send_qkv(0)
 
+    near.step(1)
+    rest.step(1)
+
     w_outer_wide[...] = w_outer[...].astype(F32)
     for k in range(8):
         w_outer_t[:, 128 * k : 128 * k + 128] = (
@@ -368,8 +376,8 @@
             .T.astype(BF16)
         )
 
-    near.step(1)
-    rest.step(1)
+    near.step(2)
+    rest.step(2)
 
     for n in range(3):
         over_x(0, n, l_all.at[x], l_all.at[from_x(n)]).wait_recv()
@@ -388,9 +396,6 @@
     place = lax.rem(source, 16) * 16 + lax.rem(lax.div(source, 16), 4) * 4 + lax.div(source, 64)
     order = jnp.where(place == target, 1.0, 0.0).astype(BF16)
     l_t[...] = jnp.dot(l_mixed[...], order, preferred_element_type=F32).astype(BF16)
-
-    near.step(2)
-    rest.step(2)
 
     own_copies[2].wait()
     for n in range(3):
@@ -467,19 +472,30 @@
             bias_block[h, g] = jnp.concatenate([v[h : h + 1] for v in offsets], axis=0)
         return carry
 
-    lax.fori_loop(0, 4, outer_rest, 0)
-
-    for h in range(2):
-        for n in range(7):
-            go(
-                over_xz(
-                    1 + h, n, bias_block.at[2 * to_xz(n) + h], bias.at[h, y, :, z, :, block_of(x)]
+    def send_bias(c):
+        half_rows = pl.ds(2 * c, 2)
+        for h in range(2):
+            for n in range(7):
+                go(
+                    over_xz(
+                        1 + 2 * c + h,
+                        n,
+                        bias_block.at[2 * to_xz(n) + h, half_rows],
+                        bias.at[h, y, half_rows, z, :, block_of(x)],
+                    )
                 )
-            )
-    own_bias = pltpu.make_async_copy(
-        bias_block.at[pl.ds(2 * x, 2)], bias.at[:, y, :, z, :, block_of(x)], own.at[4]
-    )
-    own_bias.start()
+        copy = pltpu.make_async_copy(
+            bias_block.at[pl.ds(2 * x, 2), half_rows],
+            bias.at[:, y, half_rows, z, :, block_of(x)],
+            own.at[(4, 8)[c]],
+        )
+        copy.start()
+        return copy
+
+    lax.fori_loop(0, 2, outer_rest, 0)
+    own_bias = [send_bias(0)]
+    lax.fori_loop(2, 4, outer_rest, 0)
+    own_bias.append(send_bias(1))
 
     present = jnp.concatenate([r_all[32 + k, pl.ds(pl.multiple_of(16 * yz, 16), 16), :] for k in range(4)], axis=1).astype(F32) - 1.0
     penalty[...] = jnp.concatenate(
@@ -487,12 +503,18 @@
         axis=0,
     ).astype(BF16)
 
-    def arrive_bias(h):
-        for n in range(7):
-            other_x, other_z = from_xz(n)
-            over_xz(
-                1 + h, n, bias_block.at[0], bias.at[h, y, :, other_z, :, block_of(other_x)]
-            ).wait_recv()
+    def arrive_bias(c):
+        half_rows = pl.ds(2 * c, 2)
+        own_bias[c].wait()
+        for h in range(2):
+            for n in range(7):
+                other_x, other_z = from_xz(n)
+                over_xz(
+                    1 + 2 * c + h,
+                    n,
+                    bias_block.at[0, half_rows],
+                    bias.at[h, y, half_rows, other_z, :, block_of(other_x)],
+                ).wait_recv()
 
     def bias_ring(h, c):
         def whole(b):
@@ -505,12 +527,11 @@
         return Ring(where, whole, half, ring_send.at[number], ring_recv.at[number])
 
     r0, r1, r2, r3 = [bias_ring(h, c) for h in range(2) for c in range(2)]
-    own_bias.wait()
     arrive_bias(0)
     r0.start()
+    r2.start()
+    arrive_bias(1)
     r1.start()
-    arrive_bias(1)
-    r2.start()
     r3.start()
     send_qkv(1, (2,))
 
@@ -675,13 +696,13 @@
         pltpu.VMEM((4, 2, 8, 4, 16, 128), BF16),
         dma((11, 3)),
         dma((11, 3)),
-        dma((3, 7)),
-        dma((3, 7)),
+        dma((5, 7)),
+        dma((5, 7)),
         dma((15,)),
         dma((15,)),
         dma((6, 2, 4)),
         dma((6, 2, 4)),
-        dma((8,)),
+        dma((9,)),
     ]
     gated, pair = pl.pallas_call(
         kernel,
@@ -704,7 +725,7 @@
         lookup_matrix,
         content_matrix,
         sigmoid_matrix,
-        sigmoid_offset.astype(F32).reshape(1, 256),
+        sigmoid_offset,
         first_factor_matrix.T,
         second_factor_matrix.T,
         tensor_product_matrix,

time: 115 us -> 114 us (level)
  no operation moved by 1% of the time
where the time goes in v3:
time: 114 us; the launch traced here: 113 us
  Pallas kernels  113 us (99%)
    pallas_call x1, Pallas kernels, on_device(): pl.pallas_call(kernel, name='evoformer_block', out_shape=(jax.ShapeDtypeS...  108 us
    pallas_call x1, Pallas kernels, on_device(): pl.pallas_call(finish, name='final_projection', grid=(4,), out_shape=(jax...  4.75 us

profile of v3, /device:TPU:6, one launch (start us, length us, event | category | flops | bytes accessed | tf_op | source)
XLA Modules:
  0.0 113.5 jit_solution(6186910883538151977)
XLA Ops:
  0.6 108.1 %evoformer_block.1 = (bf16[8,512,128]{2,1,0:T(8,128)(2,1)}, bf16[8,512,128]{2,1,0:T(8,128)(2,1)}) custom-call(bf16[4,512,256]{2,1,0:T(8,128)(2,1)} %hom.3, bf16[8,512,128]{2,1,0:T(8,128)(2,1)} %cpl.1, s32[4,512]{1,0:T(4,128)} %presence.1, bf16[256,256]{1,0:T(8,128)(2,1)} %w_query.1, bf16[256,256]{1,0:T(8,128)(2,1)} %w_key.1, bf16[256,256]{1,0:T(8,128)(2,1)} %w_value.1, ...), custom_call_target="tpu_custom_call" | custom-call | tf_op jit(solution)/shard_map/evoformer_block/pallas_call | solution.py:707
  108.7 4.7 %final_projection.1 = (bf16[4,512,256]{2,1,0:T(8,128)(2,1)}, bf16[8,512,128]{2,1,0:T(8,128)(2,1)}) custom-call(bf16[8,512,128]{2,1,0:T(8,128)(2,1)} %get-tuple-element.4.gated, bf16[4,512,256]{2,1,0:T(8,128)(2,1)} %hom.3, bf16[8,512,128]{2,1,0:T(8,128)(2,1)} %get-tuple-element.5.pair, bf16[256,256]{1,0:T(8,128)(2,1)} %w_final.1), custom_call_target="tpu_custom_call" | custom-call | tf_op jit(solution)/shard_map/final_projection/pallas_call | solution.py:735

commit v4 on v3

--- a/solution.py
+++ b/solution.py
@@ -158,6 +158,8 @@
     yz_recv,
     ring_send,
     ring_recv,
+    att_out,
+    att_in,
     own,
 ):
     me = lax.axis_index("dap")
@@ -408,7 +410,7 @@
 
     lax.fori_loop(0, 4, turn_couple, 0)
     near.step(3)
-    send_qkv(1, (0, 1))
+    send_qkv(1, (0,))
     rest.step(3)
     near.finish()
 
@@ -533,7 +535,7 @@
     arrive_bias(1)
     r1.start()
     r3.start()
-    send_qkv(1, (2,))
+    send_qkv(1, (1, 2))
 
     def attend(h, owner, blocks):
         count = 64 * len(blocks)
@@ -563,14 +565,24 @@
         for k, b in enumerate(blocks):
             att_send[owner, h, b] = result[k]
 
-    def run(h, offsets, after=()):
+    def back(h, n, o):
+        b = wrap(y + o, NY)
+        return remote(
+            att_send.at[to_x(n), h, b],
+            att.at[x, h, b],
+            att_out.at[h, n, o % NY],
+            att_in.at[h, n, o % NY],
+            index_of(y, to_x(n), z),
+        )
+
+    def run(h, offsets):
         blocks = [wrap(y + o, NY) for o in offsets]
 
-        def body(n, carry):
-            shift = jnp.where(n == 0, 2, jnp.where(n == 1, 1, jnp.where(n == 2, 3, 0)))
+        def body(k, carry):
+            shift = jnp.where(k == 0, 2, jnp.where(k == 1, 1, jnp.where(k == 2, 3, 0)))
             attend(h, wrap(x + shift, NX), blocks)
-            for k, action in enumerate(after):
-                pl.when(n == k)(action)
+            for slot, n in enumerate((2, 0, 1)):
+                pl.when(k == slot)(lambda n=n: perform([back(h, n, o).start for o in offsets]))
             return carry
 
         lax.fori_loop(0, 4, body, 0)
@@ -579,9 +591,6 @@
         for i in range(8):
             pair_send[g, i] = updated_t[g, i].astype(F32).T.astype(BF16)
         return carry
-
-    def back(h, n):
-        return lambda: over_x(3 + h, n, att_send.at[to_x(n), h], att.at[x, h]).start()
 
     for copy in own_qkv:
         copy.wait()
@@ -600,29 +609,33 @@
     run(0, (1, -1))
     r0.step(2)
     r1.step(2)
-    for n in range(3):
-        arrive_qkv(1, n)
-    run(1, (0, 1, -1))
     r2.step(2)
     r3.step(2)
     run(0, (2, -2))
     r0.step(3)
     r1.step(3)
-    run(1, (2, -2))
+    for n in range(3):
+        arrive_qkv(1, n)
+    run(1, (0, 1, -1))
     r2.step(3)
     r3.step(3)
+    run(1, (2, -2))
     r0.finish()
     r1.finish()
-    run(0, (3, -3, 4), (back(0, 2), back(0, 0), back(0, 1)))
+    run(0, (3, -3, 4))
     r2.finish()
     r3.finish()
-    run(1, (3, -3, 4), (back(1, 2), back(1, 0), back(1, 1)))
+    run(1, (3, -3, 4))
     own_att = pltpu.make_async_copy(att_send.at[x], att.at[x], own.at[6])
     own_att.start()
     own_att.wait()
     for h in range(2):
         for n in (2, 0, 1):
-            over_x(3 + h, n, att_send.at[0, h], att.at[from_x(n), h]).wait_recv()
+            for o in range(NY):
+                b = wrap(y + o, NY)
+                remote(
+                    att_send.at[0, h, b], att.at[from_x(n), h, b], att_out.at[h, n, o], att_in.at[h, n, o], me
+                ).wait_recv()
         for k in range(NX):
             out_gated[2 * k + h] = (att[k, h].reshape(512, 128).astype(F32) * gate[k, h]).astype(BF16)
 
@@ -631,7 +644,8 @@
         over_x(2, n, pair_send.at[0], out_pair.at[:, block_of(from_x(n)), :]).wait_recv()
     for h in range(2):
         for n in range(3):
-            over_x(3 + h, n, att_send.at[to_x(n), h], att.at[x, h]).wait_send()
+            for o in range(NY):
+                back(h, n, o).wait_send()
     for copy in sent:
         copy.wait_send()
     for one in (near, rest, r0, r1, r2, r3):
@@ -702,6 +716,8 @@
         dma((15,)),
         dma((6, 2, 4)),
         dma((6, 2, 4)),
+        dma((2, 3, 8)),
+        dma((2, 3, 8)),
         dma((9,)),
     ]
     gated, pair = pl.pallas_call(

time: 114 us -> 115 us (level)
  the two profiles are of different devices: /device:TPU:6 before, /device:TPU:128 now
where the time goes in v4:
time: 115 us; the launch traced here: 114 us
  Pallas kernels  114 us (99%)
    pallas_call x1, Pallas kernels, on_device(): pl.pallas_call(kernel, name='evoformer_block', out_shape=(jax.ShapeDtypeS...  109 us
    pallas_call x1, Pallas kernels, on_device(): pl.pallas_call(finish, name='final_projection', grid=(4,), out_shape=(jax...  4.74 us

profile of v4, /device:TPU:128, one launch (start us, length us, event | category | flops | bytes accessed | tf_op | source)
XLA Modules:
  0.0 114.4 jit_solution(9020583384682249713)
XLA Ops:
  0.6 109.0 %evoformer_block.1 = (bf16[8,512,128]{2,1,0:T(8,128)(2,1)}, bf16[8,512,128]{2,1,0:T(8,128)(2,1)}) custom-call(bf16[4,512,256]{2,1,0:T(8,128)(2,1)} %hom.3, bf16[8,512,128]{2,1,0:T(8,128)(2,1)} %cpl.1, s32[4,512]{1,0:T(4,128)} %presence.1, bf16[256,256]{1,0:T(8,128)(2,1)} %w_query.1, bf16[256,256]{1,0:T(8,128)(2,1)} %w_key.1, bf16[256,256]{1,0:T(8,128)(2,1)} %w_value.1, ...), custom_call_target="tpu_custom_call" | custom-call | tf_op jit(solution)/shard_map/evoformer_block/pallas_call | solution.py:723
  109.6 4.7 %final_projection.1 = (bf16[4,512,256]{2,1,0:T(8,128)(2,1)}, bf16[8,512,128]{2,1,0:T(8,128)(2,1)}) custom-call(bf16[8,512,128]{2,1,0:T(8,128)(2,1)} %get-tuple-element.4.gated, bf16[4,512,256]{2,1,0:T(8,128)(2,1)} %hom.3, bf16[8,512,128]{2,1,0:T(8,128)(2,1)} %get-tuple-element.5.pair, bf16[256,256]{1,0:T(8,128)(2,1)} %w_final.1), custom_call_target="tpu_custom_call" | custom-call | tf_op jit(solution)/shard_map/final_projection/pallas_call | solution.py:751

commit v5 on v3

--- a/solution.py
+++ b/solution.py
@@ -303,8 +303,6 @@
             k_send[h // 2, h % 2, pl.ds(pl.multiple_of(32 * s, 32), 32), :] = made[32 * h : 32 * h + 32]
         return carry
 
-    lax.fori_loop(0, 4, keys, 0)
-    lax.fori_loop(0, 4, heads, 0)
 
     def qkv_copies(h, n):
         other = from_x(n)
@@ -328,9 +326,6 @@
         pltpu.make_async_copy(k_send.at[x], k_got.at[x], own.at[3]),
         pltpu.make_async_copy(qv_send.at[x], qv.at[x], own.at[7]),
     ]
-    for copy in own_qkv:
-        copy.start()
-
     own_copies[0].wait()
     for n in range(7):
         other_x, other_z = from_xz(n)
@@ -364,6 +359,10 @@
         remote(l_send.at[0], l_all.at[x, from_yz], yz_send.at[n], yz_recv.at[n], me).wait_recv()
     for n in range(3):
         go(over_x(0, n, l_all.at[x], l_all.at[x]))
+    lax.fori_loop(0, 4, keys, 0)
+    lax.fori_loop(0, 4, heads, 0)
+    for copy in own_qkv:
+        copy.start()
     send_qkv(0)
 
     near.step(1)

time: 114 us -> 114 us (level)
  no operation moved by 1% of the time
where the time goes in v5:
time: 114 us; the launch traced here: 113 us
  Pallas kernels  113 us (99%)
    pallas_call x1, Pallas kernels, on_device(): pl.pallas_call(kernel, name='evoformer_block', out_shape=(jax.ShapeDtypeS...  108 us
    pallas_call x1, Pallas kernels, on_device(): pl.pallas_call(finish, name='final_projection', grid=(4,), out_shape=(jax...  4.75 us

profile of v5, /device:TPU:6, one launch (start us, length us, event | category | flops | bytes accessed | tf_op | source)
XLA Modules:
  0.0 113.5 jit_solution(1222874032178418523)
XLA Ops:
  0.6 108.1 %evoformer_block.1 = (bf16[8,512,128]{2,1,0:T(8,128)(2,1)}, bf16[8,512,128]{2,1,0:T(8,128)(2,1)}) custom-call(bf16[4,512,256]{2,1,0:T(8,128)(2,1)} %hom.3, bf16[8,512,128]{2,1,0:T(8,128)(2,1)} %cpl.1, s32[4,512]{1,0:T(4,128)} %presence.1, bf16[256,256]{1,0:T(8,128)(2,1)} %w_query.1, bf16[256,256]{1,0:T(8,128)(2,1)} %w_key.1, bf16[256,256]{1,0:T(8,128)(2,1)} %w_value.1, ...), custom_call_target="tpu_custom_call" | custom-call | tf_op jit(solution)/shard_map/evoformer_block/pallas_call | solution.py:706
  108.7 4.7 %final_projection.1 = (bf16[4,512,256]{2,1,0:T(8,128)(2,1)}, bf16[8,512,128]{2,1,0:T(8,128)(2,1)}) custom-call(bf16[8,512,128]{2,1,0:T(8,128)(2,1)} %get-tuple-element.4.gated, bf16[4,512,256]{2,1,0:T(8,128)(2,1)} %hom.3, bf16[8,512,128]{2,1,0:T(8,128)(2,1)} %get-tuple-element.5.pair, bf16[256,256]{1,0:T(8,128)(2,1)} %w_final.1), custom_call_target="tpu_custom_call" | custom-call | tf_op jit(solution)/shard_map/final_projection/pallas_call | solution.py:734

commit v6 on v4

--- a/solution.py
+++ b/solution.py
@@ -410,7 +410,7 @@
 
     lax.fori_loop(0, 4, turn_couple, 0)
     near.step(3)
-    send_qkv(1, (0,))
+    send_qkv(1, (0, 1))
     rest.step(3)
     near.finish()
 
@@ -535,7 +535,7 @@
     arrive_bias(1)
     r1.start()
     r3.start()
-    send_qkv(1, (1, 2))
+    send_qkv(1, (2,))
 
     def attend(h, owner, blocks):
         count = 64 * len(blocks)
@@ -609,17 +609,17 @@
     run(0, (1, -1))
     r0.step(2)
     r1.step(2)
+    for n in range(3):
+        arrive_qkv(1, n)
+    run(1, (0, 1, -1))
     r2.step(2)
     r3.step(2)
     run(0, (2, -2))
     r0.step(3)
     r1.step(3)
-    for n in range(3):
-        arrive_qkv(1, n)
-    run(1, (0, 1, -1))
+    run(1, (2, -2))
     r2.step(3)
     r3.step(3)
-    run(1, (2, -2))
     r0.finish()
     r1.finish()
     run(0, (3, -3, 4))

time: 115 us -> 114 us (level)
  the two profiles are of different devices: /device:TPU:128 before, /device:TPU:6 now
where the time goes in v6:
time: 114 us; the launch traced here: 113 us
  Pallas kernels  113 us (99%)
    pallas_call x1, Pallas kernels, on_device(): pl.pallas_call(kernel, name='evoformer_block', out_shape=(jax.ShapeDtypeS...  108 us
    pallas_call x1, Pallas kernels, on_device(): pl.pallas_call(finish, name='final_projection', grid=(4,), out_shape=(jax...  4.74 us

profile of v6, /device:TPU:6, one launch (start us, length us, event | category | flops | bytes accessed | tf_op | source)
XLA Modules:
  0.0 113.4 jit_solution(8065689009891217641)
XLA Ops:
  0.6 108.0 %evoformer_block.1 = (bf16[8,512,128]{2,1,0:T(8,128)(2,1)}, bf16[8,512,128]{2,1,0:T(8,128)(2,1)}) custom-call(bf16[4,512,256]{2,1,0:T(8,128)(2,1)} %hom.3, bf16[8,512,128]{2,1,0:T(8,128)(2,1)} %cpl.1, s32[4,512]{1,0:T(4,128)} %presence.1, bf16[256,256]{1,0:T(8,128)(2,1)} %w_query.1, bf16[256,256]{1,0:T(8,128)(2,1)} %w_key.1, bf16[256,256]{1,0:T(8,128)(2,1)} %w_value.1, ...), custom_call_target="tpu_custom_call" | custom-call | tf_op jit(solution)/shard_map/evoformer_block/pallas_call | solution.py:723
  108.7 4.7 %final_projection.1 = (bf16[4,512,256]{2,1,0:T(8,128)(2,1)}, bf16[8,512,128]{2,1,0:T(8,128)(2,1)}) custom-call(bf16[8,512,128]{2,1,0:T(8,128)(2,1)} %get-tuple-element.4.gated, bf16[4,512,256]{2,1,0:T(8,128)(2,1)} %hom.3, bf16[8,512,128]{2,1,0:T(8,128)(2,1)} %get-tuple-element.5.pair, bf16[256,256]{1,0:T(8,128)(2,1)} %w_final.1), custom_call_target="tpu_custom_call" | custom-call | tf_op jit(solution)/shard_map/final_projection/pallas_call | solution.py:751
